TPU v7x, 256 devices: a whole 4x4x8 slice. The times are simulated.
256 devices in a mesh: wide: 32 (over z, x), narrow: 8 (over y, core).
Axes of the slice: x: 4, y: 4, z: 8, core: 2. Of those that a mesh axis runs over, the one named last changes fastest.
Arguments:
- activations: bfloat16 [131072, 8192], P(('wide', 'narrow')), may hold values from -64 to 64
- test_matrix: bfloat16 [8192, 320], replicated, may hold values from -0.0625 to 0.0625
Outputs:
- basis: float32 [131072, 320], P(('wide', 'narrow'))
- coeffs: float32 [320, 8192], P(None, 'narrow')
All inputs are finite; a program needn't handle non-finite values.
Results may differ from a plain program's by a relative error of at most 0.00083.
Values sent between devices are 32-bit elements; how exact they have to be, the bound alone decides.
A program may use at most 128 MiB of HBM per device.

v0:
```python
import math

import jax
import jax.numpy as jnp
from jax import lax
from jax.sharding import PartitionSpec as P


def per_device(activations, test_matrix):
    n_wide = lax.axis_size("wide")
    n_narrow = lax.axis_size("narrow")
    total_rows = activations.shape[0] * n_wide * n_narrow
    sketch = jnp.dot(activations, test_matrix, preferred_element_type=jnp.float32)
    gram_local = jnp.dot(sketch.T, sketch, precision=lax.Precision.HIGHEST)
    gram = lax.psum(gram_local, ("wide", "narrow"))
    lower_factor = jnp.linalg.cholesky(gram)
    basis = lax.linalg.triangular_solve(
        lower_factor, sketch, left_side=False, lower=True, transpose_a=True
    ) * math.sqrt(total_rows)
    basis_half = basis.astype(jnp.bfloat16)
    partial_sum = lax.dot_general(
        basis_half, activations, (((0,), (0,)), ((), ())), preferred_element_type=jnp.float32
    )
    share = lax.psum_scatter(partial_sum, "narrow", scatter_dimension=1, tiled=True)
    summed = lax.psum(share, "wide")
    coeffs = summed / total_rows
    return (basis, coeffs)


def solution(mesh):
    placed = (P(("wide", "narrow"), None), P())
    return jax.shard_map(
        per_device,
        mesh=mesh,
        in_specs=placed,
        out_specs=(P(("wide", "narrow"), None), P(None, "narrow")),
        check_vma=False,
    )
```

profile of v0, /device:TPU:8, one launch (start us, length us, event | category | flops | bytes accessed | tf_op | source)
XLA Modules:
  0.0 601.0 jit_solution(5530297213288675070)
XLA Ops:
  7.2 10.1 %fusion.22 = f32[512,320]{0,1:T(8,128)S(1)} fusion(bf16[512,8192]{1,0:T(8,128)(2,1)} %param.2, bf16[8192,320]{0,1:T(8,128)(2,1)} %param.3), kind=kOutput, calls=%fused_computation.57 | convolution fusion | flops 2684354560 | bytes 14286848 | tf_op jit(solution)/shard_map/dot_general | solution.py:13
  17.3 2.0 fusion.23
  19.3 0.2 reduce-scatter.2.cloned.1.call-start
  19.6 255.2 %all-reduce.6.cloned.1.call-done = f32[320,320]{0,1:T(8,128)} async-done(((f32[320,320]{0,1:T(8,128)}), f32[320,320]{0,1:T(8,128)}) %all-reduce.6.cloned.1.call-update) | async-done | bytes 409616 | tf_op jit(solution)/shard_map/psum | solution.py:15
  274.8 1.2 copy.5
  276.0 1.1 fusion.3
  277.1 11.7 %cholesky.78 = f32[128,128]{1,0:T(8,128)S(1)} custom-call(f32[128,128]{1,0:T(8,128)S(1)} %cholesky.198), custom_call_target="Cholesky" | custom-call | tf_op jit(solution)/shard_map/jit(cholesky)/cholesky | solution.py:16
  288.9 9.8 %custom-call.22 = f32[1,128,128]{1,2,0:T(8,128)S(1)} custom-call(f32[1,128,128]{2,1,0:T(8,128)S(1)} %get-tuple-element.24), custom_call_target="InvertDiagBlocksLowerTriangular" | custom-call | tf_op jit(solution)/shard_map/jit(cholesky)/cholesky | solution.py:16
  298.7 0.2 constant_dynamic-update-slice_fusion.2
  299.0 0.3 convolution_subtract_fusion.2
  299.3 11.7 %cholesky.164 = f32[128,128]{1,0:T(8,128)S(1)} custom-call(f32[128,128]{1,0:T(8,128)S(1)} %cholesky.202), custom_call_target="Cholesky" | custom-call | tf_op jit(solution)/shard_map/jit(cholesky)/cholesky | solution.py:16
  311.0 10.0 %custom-call.23 = f32[1,128,128]{1,2,0:T(8,128)S(1)} custom-call(f32[1,128,128]{2,1,0:T(8,128)S(1)} %get-tuple-element.21), custom_call_target="InvertDiagBlocksLowerTriangular" | custom-call | tf_op jit(solution)/shard_map/jit(cholesky)/cholesky | solution.py:16
  321.0 0.2 convolution_dynamic-update-slice_fusion
  321.2 0.2 convolution_subtract_fusion.3
  321.4 5.8 cholesky.186
  327.3 0.7 compare_reduce_fusion
  328.0 0.6 compare_reduce_fusion.1
  330.8 4.0 while.1
  330.8 0.6 fusion.34
  331.4 1.4 bitcast_dynamic-update-slice_fusion.2
  332.8 0.6 fusion.34
  333.4 1.4 bitcast_dynamic-update-slice_fusion.2
  334.9 29.5 %custom-call.24 = f32[3,128,128]{1,2,0:T(8,128)S(1)} custom-call(f32[3,128,128]{2,1,0:T(8,128)S(1)} %pad_maximum_fusion), custom_call_target="InvertDiagBlocksLowerTriangular" | custom-call | tf_op jit(solution)/shard_map/triangular_solve | solution.py:17
  364.4 0.4 fusion.6
  364.8 0.4 convolution_subtract_fusion
  365.2 0.4 fusion.11
  365.6 0.5 convolution_subtract_fusion.1
  366.1 0.3 fusion.18
  366.5 9.2 %fusion.4 = f32[320,8192]{1,0:T(8,128)} fusion(bf16[512,8192]{1,0:T(8,128)(2,1)} %param.2, f32[512,320]{0,1:T(8,128)S(1)} %maximum_multiply_fusion), kind=kOutput, calls=%fused_computation.16 | convolution fusion | flops 2684518400 | bytes 19529728 | tf_op jit(solution)/shard_map/dot_general | solution.py:21
  375.7 59.8 %reduce-scatter.2.cloned.1.call-done = f32[320,1024]{1,0:T(8,128)} async-done(((f32[320,8192]{1,0:T(8,128)}), f32[320,1024]{1,0:T(8,128)}) %reduce-scatter.2.cloned.1.call-update) | async-done | bytes 1310736 | tf_op jit(solution)/shard_map/reduce_scatter | solution.py:24
  435.6 156.3 %all-reduce.8.cloned.1.call-done = f32[320,1024]{1,0:T(8,128)} async-done(((f32[320,1024]{1,0:T(8,128)}), f32[320,1024]{1,0:T(8,128)}) %all-reduce.8.cloned.1.call-update) | async-done | bytes 1310736 | tf_op jit(solution)/shard_map/psum | solution.py:25
  591.9 2.5 broadcast_multiply_fusion
  (25 shorter events, 0.6 us)
Async XLA Ops:
  7.2 267.6 %all-reduce.6.cloned.1.call-start = ((), (), s32[]{:S(2)}) async-start(), calls=%async_computation.1 | async-start | bytes 983040 | tf_op jit(solution)/shard_map/psum | solution.py:15
  19.3 416.3 %reduce-scatter.2.cloned.1.call-start = ((), (), s32[]{:S(2)}) async-start(), calls=%async_computation.2 | async-start | bytes 11796480 | tf_op jit(solution)/shard_map/reduce_scatter | solution.py:24
  366.5 9.2 %copy-start = (f32[512,320]{0,1:T(8,128)}, f32[512,320]{0,1:T(8,128)S(1)}, u32[]{:S(2)}) copy-start(f32[512,320]{0,1:T(8,128)S(1)} %maximum_multiply_fusion) | copy-start | bytes 1966084
  375.7 216.2 %all-reduce.8.cloned.1.call-start = ((), (), s32[]{:S(2)}) async-start(), calls=%async_computation.3 | async-start | bytes 2621440 | tf_op jit(solution)/shard_map/psum | solution.py:25
Sparse Core Ops, SparseCore 0:
  19.4 255.3 all-reduce.5
  375.8 59.7 reduce-scatter.1
  439.0 152.8 all-reduce.7
where the time goes:
time: 601 us
  waiting for transfers between devices  471 us (78%)
  other arithmetic  83.9 us (14%)
  matrix products  24.1 us (4%)
  between operations  15.9 us (3%)
    psum x1, waiting for transfers between devices, per_device(): gram = lax.psum(gram_local, ('wide', 'narrow'))  255 us
    psum x1, waiting for transfers between devices, per_device(): summed = lax.psum(share, 'wide')  156 us
    reduce_scatter x1, waiting for transfers between devices, per_device(): lax.psum_scatter(partial_sum, 'narrow', scatter_dimension=1, tiled=True)  59.8 us
    another operation x10, other arithmetic, per_device(): lower_factor = jnp.linalg.cholesky(gram)  50.5 us
    another operation x7, other arithmetic, per_device(): lax.linalg.triangular_solve(lower_factor, sketch, left_side=False, lower=...  29.7 us
  transfers between devices with their start and end apart: 3, of which 3 were waited for; matrix products, arithmetic and copies ran while one was open for 0% of the time, Pallas kernels for 0%

commit v1 on v0

v1 whole, which is shorter than its diff:
```python
import functools
import math

import jax
import jax.numpy as jnp
from jax import lax
from jax.experimental import pallas as pl
from jax.experimental.pallas import tpu as pltpu
from jax.sharding import PartitionSpec as P

MESH = pl.DeviceIdType.MESH
HIGHEST = lax.Precision.HIGHEST
F32 = jnp.float32
BF16 = jnp.bfloat16
NX, NY, NZ = 4, 4, 8
BLOCK = 64
LANES = 128

CHUNKS = (("y", 0, 96), ("y", 96, 96), ("x", 192, 64), ("z", 256, 64))


def inverse_factor_block(block):
    n = block.shape[0]
    rows = lax.broadcasted_iota(jnp.int32, (n, n), 0)
    cols = lax.broadcasted_iota(jnp.int32, (n, n), 1)
    state = jnp.concatenate([block, jnp.where(rows == cols, 1.0, 0.0).astype(F32)], axis=1)
    row_in_group = lax.broadcasted_iota(jnp.int32, (8, 2 * n), 0)
    done = []
    for group in range(n // 8):
        left = n - 8 * group
        head = state[0:8, :]
        columns = [
            jnp.broadcast_to(state[:, 8 * group + j : 8 * group + j + 1], (left, 2 * n))
            for j in range(8)
        ]
        pivot_rows, pivot_cols = [], []
        for j in range(8):
            inv = lax.rsqrt(columns[j][j : j + 1, :])
            row = head[j : j + 1, :] * inv
            col = columns[j] * inv
            pivot_rows.append(row)
            pivot_cols.append(col)
            if j < 7:
                head = head - col[0:8] * row
            for later in range(j + 1, 8):
                columns[later] = columns[later] - col * col[later : later + 1, :]
        out = jnp.broadcast_to(pivot_rows[0], (8, 2 * n))
        for j in range(1, 8):
            out = jnp.where(row_in_group == j, pivot_rows[j], out)
        done.append(out)
        if left > 8:
            state = state[8:, :]
            for j in range(8):
                state = state - pivot_cols[j][8:] * pivot_rows[j]
    return jnp.concatenate(done, axis=0)[:, n:]


def factor_step(m_ref, step):
    k = m_ref.shape[0]
    lo, hi = step * BLOCK, (step + 1) * BLOCK
    inverse = inverse_factor_block(m_ref[lo:hi, lo:hi])
    rows = lax.broadcasted_iota(jnp.int32, (BLOCK, BLOCK), 0)
    cols = lax.broadcasted_iota(jnp.int32, (BLOCK, BLOCK), 1)
    m_ref[lo:hi, lo:hi] = jnp.where(rows == cols, 1.0, 0.0).astype(F32)
    panel = jnp.dot(inverse, m_ref[lo:hi, :], precision=HIGHEST, preferred_element_type=F32)
    m_ref[lo:hi, :] = panel
    if hi < k:
        m_ref[hi:, lo:hi] = jnp.zeros((k - hi, BLOCK), F32)
        m_ref[hi:, :] -= lax.dot_general(
            panel[:, hi:], panel, (((0,), (0,)), ((), ())),
            precision=HIGHEST, preferred_element_type=F32,
        )


def kernel(n_total, a_hbm, om_hbm, basis_ref, coef_ref,
           a_buf, om_buf, sketch, halves, to_core, from_core, part, total,
           folded, g_core, g_plane, g_line, g_sum, mat, load_sem, sems, *bufs):
    k = sketch.shape[1]
    wide, narrow = lax.axis_index("wide"), lax.axis_index("narrow")
    x, z = lax.rem(wide, NX), wide // NX
    y, c = narrow // 2, lax.rem(narrow, 2)

    def device(xx, yy, zz, cc):
        return (zz * NX + xx, yy * 2 + cc)

    sibling = device(x, y, z, 1 - c)
    on_x = [(lax.rem(x + d, NX), device(lax.rem(x + d, NX), y, z, c)) for d in range(1, NX)]
    on_y = [(lax.rem(y + d, NY), device(x, lax.rem(y + d, NY), z, c)) for d in range(1, NY)]
    on_z = [(lax.rem(z + d, NZ), device(x, y, lax.rem(z + d, NZ), c)) for d in range(1, NZ)]
    place = y * NX + x
    on_plane = []
    for d in range(1, NX * NY):
        other = lax.rem(place + d, NX * NY)
        on_plane.append((other, device(lax.rem(other, NX), other // NX, z, c)))

    used = [0]
    pending = []

    def exchange(size_like):
        at = used[0]
        used[0] += 2
        pending.append((at, size_like))
        return at

    def send(at, src, dst, to):
        pltpu.make_async_remote_copy(
            src_ref=src, dst_ref=dst, send_sem=sems.at[at], recv_sem=sems.at[at + 1],
            device_id=to, device_id_type=MESH,
        ).start()

    def wait_bytes(sem, like):
        pltpu.make_async_copy(like, like, sem).wait()

    def received(at, like):
        wait_bytes(sems.at[at + 1], like)

    barrier = pltpu.get_barrier_semaphore()
    partners = [sibling] + [to for _, to in on_plane] + [to for _, to in on_z]
    n_blocks, _, width = a_buf.shape
    loads = []
    for j in range(n_blocks):
        loads.append((
            pltpu.make_async_copy(a_hbm.at[:, pl.ds(j * width, width)], a_buf.at[j], load_sem.at[j]),
            pltpu.make_async_copy(om_hbm.at[pl.ds(j * width, width), :], om_buf.at[j], load_sem.at[n_blocks + j]),
        ))
    for first, second in loads:
        first.start()
        second.start()
    for to in partners:
        pl.semaphore_signal(barrier, inc=1, device_id=to, device_id_type=MESH)

    for j in range(n_blocks):
        loads[j][0].wait()
        loads[j][1].wait()
        term = jnp.dot(a_buf[j], om_buf[j], preferred_element_type=F32)
        if j == 0:
            sketch[...] = term
        else:
            sketch[...] += term

    gram = lax.dot_general(
        sketch[...], sketch[...], (((0,), (0,)), ((), ())),
        precision=HIGHEST, preferred_element_type=F32,
    )
    folded[...] = jnp.zeros(folded.shape, F32)
    folded[0:128, 0:k] = gram[0:128, :]
    folded[128:256, 0 : k - 128] = gram[128:256, 128:]
    folded[128 : k - 128, 256 : k] = gram[256:, 256:]

    pl.semaphore_wait(barrier, len(partners))
    half_rows = g_core.shape[0]
    mine = pl.multiple_of(c * half_rows, 8)
    yours = pl.multiple_of((1 - c) * half_rows, 8)
    ex_core = exchange(g_core)
    send(ex_core, folded.at[pl.ds(yours, half_rows)], g_core, sibling)

    value = sketch[...]
    high = value.astype(BF16)
    low = (value - high.astype(F32)).astype(BF16)
    halves[0:k, :] = high.T
    halves[k:, :] = low.T

    def project(block, dst, at):
        def columns(q, carry):
            cols = pl.ds(pl.multiple_of(q * 256, 256), 256)
            res = jnp.dot(halves[...], a_buf[block, :, cols], preferred_element_type=F32)
            res = res[0:k] + res[k:]
            dst[at, 2 * q] = res[:, 0:LANES]
            dst[at, 2 * q + 1] = res[:, LANES:]
            return carry

        lax.fori_loop(0, width // 256, columns, 0)

    owners = [lax.rem(y + d, NY) for d in (1, 2, 3, 0)]
    ex_owner = []
    for i, o in enumerate(owners):
        project(2 * o + 1 - c, to_core, o)
        at = exchange(from_core.at[o])
        ex_owner.append(at)
        send(at, to_core.at[o], from_core.at[o], sibling)
        project(2 * o + c, part, o)
        if i == 0:
            received(ex_core, g_core)
            folded[pl.ds(mine, half_rows)] += g_core[...]
            my_tile = pl.multiple_of(c * half_rows + place * 8, 8)
            ex_plane = exchange(g_plane)
            for d, (other, to) in enumerate(on_plane):
                src = folded.at[pl.ds(pl.multiple_of(c * half_rows + other * 8, 8), 8)]
                send(ex_plane, src, g_plane.at[d], to)

    class Chunk:
        pass

    chunks = []
    for i, (axis, first, n) in enumerate(CHUNKS):
        ch = Chunk()
        ch.axis, ch.first, ch.n, ch.q = axis, first, n, n // NX
        ch.b1, ch.b2, ch.b3 = bufs[3 * i : 3 * i + 3]
        ch.rows = pl.ds(first, n)
        ch.mine = pl.ds(pl.multiple_of(first + x * ch.q, 8), ch.q)
        ch.ex1 = exchange(ch.b1)
        chunks.append(ch)

    def quarter(ch, xx):
        return pl.ds(pl.multiple_of(ch.first + xx * ch.q, 8), ch.q)

    def first_sends(ch, i, o):
        if ch.axis == "y":
            if i < NY - 1:
                send(ch.ex1, part.at[o, :, ch.rows, :], ch.b1.at[i], on_y[i][1])
        elif ch.axis == "x":
            for d, (xx, to) in enumerate(on_x):
                send(ch.ex1, part.at[o, :, quarter(ch, xx), :], ch.b1.at[d, o], to)
        else:
            for d, (zz, to) in enumerate(on_z):
                send(ch.ex1, part.at[o, zz, ch.rows, :], ch.b1.at[d, o], to)

    def summed(buf, n):
        acc = buf[0]
        for d in range(1, n):
            acc = acc + buf[d]
        return acc

    def second(ch):
        received(ch.ex1, ch.b1)
        ch.ex2 = exchange(ch.b2)
        if ch.axis == "y":
            def add(t, carry):
                part[y, t, ch.rows, :] += ch.b1[0, t] + ch.b1[1, t] + ch.b1[2, t]
                return carry

            lax.fori_loop(0, NZ, add, 0)
            for d, (xx, to) in enumerate(on_x):
                send(ch.ex2, part.at[y, :, quarter(ch, xx), :], ch.b2.at[d], to)
        elif ch.axis == "x":
            def add(o, carry):
                part[o, :, ch.mine, :] += ch.b1[0, o] + ch.b1[1, o] + ch.b1[2, o]
                return carry

            lax.fori_loop(0, NY, add, 0)
            for d, (yy, to) in enumerate(on_y):
                send(ch.ex2, part.at[yy, :, ch.mine, :], ch.b2.at[d], to)
        else:
            def add(o, carry):
                acc = part[o, z, ch.rows, :]
                for d in range(NZ - 1):
                    acc = acc + ch.b1[d, o]
                part[o, z, ch.rows, :] = acc
                return carry

            lax.fori_loop(0, NY, add, 0)
            for d, (yy, to) in enumerate(on_y):
                send(ch.ex2, part.at[yy, z, ch.rows, :], ch.b2.at[d], to)

    def third(ch):
        received(ch.ex2, ch.b2)
        ch.ex3 = exchange(ch.b3)
        if ch.axis == "z":
            part[y, z, ch.rows, :] += summed(ch.b2, NY - 1)
            for d, (xx, to) in enumerate(on_x):
                send(ch.ex3, part.at[y, z, quarter(ch, xx), :], ch.b3.at[d], to)
        else:
            part[y, :, ch.mine, :] += summed(ch.b2, 3)
            for d, (zz, to) in enumerate(on_z):
                send(ch.ex3, part.at[y, zz, ch.mine, :], ch.b3.at[d], to)

    def fourth(ch):
        received(ch.ex3, ch.b3)
        total[z, ch.mine, :] = part[y, z, ch.mine, :] + summed(ch.b3, ch.b3.shape[0])
        ch.ex4 = exchange(total.at[pl.ds(0, NZ - 1), pl.ds(0, ch.q), :])
        for _, to in on_z:
            send(ch.ex4, total.at[z, ch.mine, :], total.at[z, ch.mine, :], to)

    def fifth(ch):
        received(ch.ex4, total.at[pl.ds(0, NZ - 1), pl.ds(0, ch.q), :])
        ch.ex5 = exchange(total.at[:, pl.ds(0, 3 * ch.q), :])
        for _, to in on_x:
            send(ch.ex5, total.at[:, ch.mine, :], total.at[:, ch.mine, :], to)

    def last(ch):
        received(ch.ex5, total.at[:, pl.ds(0, 3 * ch.q), :])

    def owner_ready(i):
        o = owners[i]
        received(ex_owner[i], from_core.at[o])

        def add(t, carry):
            part[o, t] += from_core[o, t]
            return carry

        lax.fori_loop(0, NZ, add, 0)
        for ch in chunks:
            first_sends(ch, i, o)

    tile = pl.ds(my_tile, 8)

    def gram_line():
        received(ex_plane, g_plane)
        g_line[z] = folded[tile, :] + summed(g_plane, NX * NY - 1)
        at = exchange(g_plane.at[pl.ds(0, NZ - 1)])
        for _, to in on_z:
            send(at, g_line.at[z], g_line.at[z], to)
        return at

    def gram_spread(at):
        received(at, g_plane.at[pl.ds(0, NZ - 1)])
        g_sum[tile, :] = summed(g_line, NZ)
        at = exchange(g_plane)
        for _, to in on_plane:
            send(at, g_sum.at[tile], g_sum.at[tile], to)
        return at

    def gram_core(at):
        received(at, g_plane)
        at = exchange(g_core)
        my_half = pl.ds(mine, half_rows)
        send(at, g_sum.at[my_half], g_sum.at[my_half], sibling)
        return at

    def gram_ready(at):
        received(at, g_core)
        mat[0:128, :] = g_sum[0:128, 0:k]
        mat[128:256, 128:] = g_sum[128:256, 0 : k - 128]
        mat[256:, 256:] = g_sum[128 : k - 128, 256 : k]

    y0, y1, xc, zc = chunks
    owner_ready(0)
    owner_ready(1)
    at = gram_line()
    owner_ready(2)
    owner_ready(3)
    at = gram_spread(at)
    at = gram_core(at)
    second(xc)
    gram_ready(at)
    factor_step(mat, 0)
    third(xc)
    second(y0)
    factor_step(mat, 1)
    fourth(xc)
    third(y0)
    factor_step(mat, 2)
    fifth(xc)
    second(zc)
    factor_step(mat, 3)
    fourth(y0)
    third(zc)
    factor_step(mat, 4)
    rows = lax.broadcasted_iota(jnp.int32, (k, k), 0)
    cols = lax.broadcasted_iota(jnp.int32, (k, k), 1)
    mat[...] = jnp.where(rows >= cols, mat[...], 0.0)
    second(y1)
    fifth(y0)
    fourth(zc)
    basis_ref[...] = lax.dot_general(
        sketch[...], mat[...], (((1,), (1,)), ((), ())),
        precision=HIGHEST, preferred_element_type=F32,
    ) * math.sqrt(n_total)
    third(y1)
    fifth(zc)
    fourth(y1)
    fifth(y1)
    for ch in chunks:
        last(ch)

    def finish(q, carry):
        cols = pl.ds(pl.multiple_of(q * 256, 256), 256)
        both = jnp.concatenate([total[2 * q], total[2 * q + 1]], axis=1)
        coef_ref[:, cols] = jnp.dot(
            mat[...], both, precision=HIGHEST, preferred_element_type=F32
        ) * (1.0 / math.sqrt(n_total))
        return carry

    lax.fori_loop(0, coef_ref.shape[1] // 256, finish, 0)
    for at, like in pending:
        wait_bytes(sems.at[at], like)


def per_device(activations, test_matrix):
    rows, d = activations.shape
    k = test_matrix.shape[1]
    n_total = rows * lax.axis_size("wide") * lax.axis_size("narrow")
    width = d // (2 * NY)
    bufs = []
    for axis, _, n in CHUNKS:
        q = n // NX
        if axis == "y":
            shapes = ((3, NZ, n, LANES), (3, NZ, q, LANES), (7, q, LANES))
        elif axis == "x":
            shapes = ((3, NY, NZ, q, LANES), (3, NZ, q, LANES), (7, q, LANES))
        else:
            shapes = ((7, NY, n, LANES), (3, n, LANES), (3, q, LANES))
        bufs += [pltpu.VMEM(s, F32) for s in shapes]
    block = (NY, NZ, k, LANES)
    return pl.pallas_call(
        functools.partial(kernel, n_total),
        out_shape=(
            jax.ShapeDtypeStruct((rows, k), F32),
            jax.ShapeDtypeStruct((k, width), F32),
        ),
        in_specs=[pl.BlockSpec(memory_space=pl.ANY)] * 2,
        out_specs=(pl.BlockSpec(memory_space=pltpu.VMEM), pl.BlockSpec(memory_space=pltpu.VMEM)),
        scratch_shapes=[
            pltpu.VMEM((d // width, rows, width), BF16),
            pltpu.VMEM((d // width, width, k), BF16),
            pltpu.VMEM((rows, k), F32),
            pltpu.VMEM((2 * k, rows), BF16),
            pltpu.VMEM(block, F32),
            pltpu.VMEM(block, F32),
            pltpu.VMEM(block, F32),
            pltpu.VMEM((NZ, k, LANES), F32),
            pltpu.VMEM((256, 384), F32),
            pltpu.VMEM((128, 384), F32),
            pltpu.VMEM((NX * NY - 1, 8, 384), F32),
            pltpu.VMEM((NZ, 8, 384), F32),
            pltpu.VMEM((256, 384), F32),
            pltpu.VMEM((k, k), F32),
            pltpu.SemaphoreType.DMA((2 * d // width,)),
            pltpu.SemaphoreType.DMA((64,)),
        ] + bufs,
        compiler_params=pltpu.CompilerParams(
            collective_id=0, has_side_effects=True, vmem_limit_bytes=56 * 1024 * 1024
        ),
        name="range_finder",
    )(activations, test_matrix)


def solution(mesh):
    return jax.shard_map(
        per_device,
        mesh=mesh,
        in_specs=(P(("wide", "narrow"), None), P()),
        out_specs=(P(("wide", "narrow"), None), P(None, "narrow")),
        check_vma=False,
    )
```

time: 601 us -> 125 us (0.21)
  waiting for transfers between devices: 471 us -> 0 us
  Pallas kernels: 0 us -> 111 us
  other arithmetic: 83.9 us -> 0 us
  matrix products: 24.1 us -> 0 us
  between operations: 15.9 us -> 0.64 us
  local copies, waits for them, and re-layouts: 5.32 us -> 12.9 us
    psum x2 -> x0, waiting for transfers between devices: 412 us -> none  [the longest x1 255 us: per_device(): gram = lax.psum(gram_local, ('wide', 'narrow'))]
    pallas_call x0 -> x1, Pallas kernels: none -> 111 us  [per_device(): pl.pallas_call(functools.partial(kernel, n_total), out_shape=(jax.ShapeDt...]
    another operation x17 -> x0, other arithmetic: 80.2 us -> none  [the longest x10 50.5 us: per_device(): lower_factor = jnp.linalg.cholesky(gram)]
    reduce_scatter x1 -> x0, waiting for transfers between devices: 59.8 us -> none  [per_device(): lax.psum_scatter(partial_sum, 'narrow', scatter_dimension=1, tiled=True)]
    dot_general x3 -> x0, matrix products: 21.2 us -> none  [the longest x1 10.1 us: per_device(): jnp.dot(activations, test_matrix, preferred_element_type=jnp.float32)]
    unnamed x2, local copies, waits for them, and re-layouts: 0.01 us -> 10.7 us
  transfers between devices with their start and end apart: 3 -> 0, of which waited for: 3 -> 0; matrix products, arithmetic and copies ran while one was open for 0% -> 0% of each run, Pallas kernels for 0% -> 0%
where the time goes in v1:
time: 125 us
  Pallas kernels  111 us (89%)
  local copies, waits for them, and re-layouts  12.9 us (10%)
    pallas_call x1, Pallas kernels, per_device(): pl.pallas_call(functools.partial(kernel, n_total), out_shape=(jax.ShapeDt...  111 us
    unnamed x2, local copies, waits for them, and re-layouts  10.7 us

profile of v1, /device:TPU:8, one launch (start us, length us, event | category | flops | bytes accessed | tf_op | source)
XLA Modules:
  0.0 125.0 jit_solution(7740222500530932471)
XLA Ops:
  0.6 8.2 %copy.4.om_hbm = bf16[8192,320]{1,0:T(8,128)(2,1)} copy(bf16[8192,320]{0,1:T(8,128)(2,1)} %param.3) | data formatting | bytes 10485760 | tf_op args[1]
  8.8 111.5 %range_finder.1 = (f32[512,320]{1,0:T(8,128)}, f32[320,1024]{1,0:T(8,128)}) custom-call(bf16[512,8192]{1,0:T(8,128)(2,1)} %a_hbm.1, bf16[8192,320]{1,0:T(8,128)(2,1)} %copy.4.om_hbm), custom_call_target="tpu_custom_call" | custom-call | tf_op jit(solution)/shard_map/range_finder/pallas_call | solution.py:395
  120.3 2.2 %copy.5 = f32[512,320]{0,1:T(8,128)} copy(f32[512,320]{1,0:T(8,128)} %get-tuple-element.2) | data formatting | bytes 1310720 | tf_op jit(solution)/shard_map/range_finder/pallas_call | solution.py:395
  122.5 2.5 %copy.7 = f32[320,1024]{1,0:T(8,128)} copy(f32[320,1024]{1,0:T(8,128)} %get-tuple-element.7) | data formatting | bytes 2621440

commit v2 on v1

--- a/solution.py
+++ b/solution.py
@@ -72,10 +72,10 @@
         )
 
 
-def kernel(n_total, a_hbm, om_hbm, basis_ref, coef_ref,
+def kernel(n_total, a_hbm, om_hbm, basis_hbm, total_hbm, inv_hbm,
            a_buf, om_buf, sketch, halves, to_core, from_core, part, total,
-           folded, g_core, g_plane, g_line, g_sum, mat, load_sem, sems, *bufs):
-    k = sketch.shape[1]
+           folded, g_core, g_plane, g_line, g_sum, mat, basis_t, load_sem, out_sem, sems, *bufs):
+    rows_here, k = sketch.shape
     wide, narrow = lax.axis_index("wide"), lax.axis_index("narrow")
     x, z = lax.rem(wide, NX), wide // NX
     y, c = narrow // 2, lax.rem(narrow, 2)
@@ -121,7 +121,7 @@
     for j in range(n_blocks):
         loads.append((
             pltpu.make_async_copy(a_hbm.at[:, pl.ds(j * width, width)], a_buf.at[j], load_sem.at[j]),
-            pltpu.make_async_copy(om_hbm.at[pl.ds(j * width, width), :], om_buf.at[j], load_sem.at[n_blocks + j]),
+            pltpu.make_async_copy(om_hbm.at[:, pl.ds(j * width, width)], om_buf.at[j], load_sem.at[n_blocks + j]),
         ))
     for first, second in loads:
         first.start()
@@ -132,7 +132,9 @@
     for j in range(n_blocks):
         loads[j][0].wait()
         loads[j][1].wait()
-        term = jnp.dot(a_buf[j], om_buf[j], preferred_element_type=F32)
+        term = lax.dot_general(
+            a_buf[j], om_buf[j], (((1,), (1,)), ((), ())), preferred_element_type=F32
+        )
         if j == 0:
             sketch[...] = term
         else:
@@ -157,36 +159,31 @@
     value = sketch[...]
     high = value.astype(BF16)
     low = (value - high.astype(F32)).astype(BF16)
-    halves[0:k, :] = high.T
-    halves[k:, :] = low.T
+    halves[:, 0:rows_here] = high.T
+    halves[:, rows_here:] = low.T
 
     def project(block, dst, at):
-        def columns(q, carry):
-            cols = pl.ds(pl.multiple_of(q * 256, 256), 256)
-            res = jnp.dot(halves[...], a_buf[block, :, cols], preferred_element_type=F32)
-            res = res[0:k] + res[k:]
-            dst[at, 2 * q] = res[:, 0:LANES]
-            dst[at, 2 * q + 1] = res[:, LANES:]
-            return carry
-
-        lax.fori_loop(0, width // 256, columns, 0)
+        cols = a_buf[block]
+        res = jnp.dot(
+            halves[...], jnp.concatenate([cols, cols], axis=0), preferred_element_type=F32
+        )
+        for t in range(NZ):
+            dst[at, t] = res[:, t * LANES : (t + 1) * LANES]
 
     owners = [lax.rem(y + d, NY) for d in (1, 2, 3, 0)]
     ex_owner = []
-    for i, o in enumerate(owners):
+    for o in owners:
         project(2 * o + 1 - c, to_core, o)
         at = exchange(from_core.at[o])
         ex_owner.append(at)
         send(at, to_core.at[o], from_core.at[o], sibling)
-        project(2 * o + c, part, o)
-        if i == 0:
-            received(ex_core, g_core)
-            folded[pl.ds(mine, half_rows)] += g_core[...]
-            my_tile = pl.multiple_of(c * half_rows + place * 8, 8)
-            ex_plane = exchange(g_plane)
-            for d, (other, to) in enumerate(on_plane):
-                src = folded.at[pl.ds(pl.multiple_of(c * half_rows + other * 8, 8), 8)]
-                send(ex_plane, src, g_plane.at[d], to)
+    received(ex_core, g_core)
+    folded[pl.ds(mine, half_rows)] += g_core[...]
+    my_tile = pl.multiple_of(c * half_rows + place * 8, 8)
+    ex_plane = exchange(g_plane)
+    for d, (other, to) in enumerate(on_plane):
+        src = folded.at[pl.ds(pl.multiple_of(c * half_rows + other * 8, 8), 8)]
+        send(ex_plane, src, g_plane.at[d], to)
 
     class Chunk:
         pass
@@ -282,6 +279,7 @@
 
     def owner_ready(i):
         o = owners[i]
+        project(2 * o + c, part, o)
         received(ex_owner[i], from_core.at[o])
 
         def add(t, carry):
@@ -352,28 +350,48 @@
     second(y1)
     fifth(y0)
     fourth(zc)
-    basis_ref[...] = lax.dot_general(
-        sketch[...], mat[...], (((1,), (1,)), ((), ())),
+    basis_t[...] = lax.dot_general(
+        mat[...], sketch[...], (((1,), (1,)), ((), ())),
         precision=HIGHEST, preferred_element_type=F32,
     ) * math.sqrt(n_total)
+    outs = [
+        pltpu.make_async_copy(mat, inv_hbm, out_sem.at[0]),
+        pltpu.make_async_copy(basis_t, basis_hbm, out_sem.at[1]),
+    ]
+    for copy in outs:
+        copy.start()
     third(y1)
     fifth(zc)
     fourth(y1)
     fifth(y1)
-    for ch in chunks:
+    for i, ch in enumerate(chunks):
         last(ch)
-
-    def finish(q, carry):
-        cols = pl.ds(pl.multiple_of(q * 256, 256), 256)
-        both = jnp.concatenate([total[2 * q], total[2 * q + 1]], axis=1)
-        coef_ref[:, cols] = jnp.dot(
-            mat[...], both, precision=HIGHEST, preferred_element_type=F32
-        ) * (1.0 / math.sqrt(n_total))
-        return carry
-
-    lax.fori_loop(0, coef_ref.shape[1] // 256, finish, 0)
+        copy = pltpu.make_async_copy(
+            total.at[:, ch.rows, :], total_hbm.at[:, ch.rows, :], out_sem.at[2 + i]
+        )
+        copy.start()
+        outs.append(copy)
+    for copy in outs:
+        copy.wait()
     for at, like in pending:
         wait_bytes(sems.at[at], like)
+
+
+def finish_kernel(n_total, steps, basis_hbm, total_ref, inv_ref, basis_out, coef_ref, sem):
+    copy = pltpu.make_async_copy(basis_hbm, basis_out, sem)
+
+    @pl.when(pl.program_id(0) == 0)
+    def _():
+        copy.start()
+
+    both = jnp.concatenate([total_ref[0], total_ref[1]], axis=1)
+    coef_ref[...] = jnp.dot(
+        inv_ref[...], both, precision=HIGHEST, preferred_element_type=F32
+    ) * (1.0 / math.sqrt(n_total))
+
+    @pl.when(pl.program_id(0) == steps - 1)
+    def _():
+        copy.wait()
 
 
 def per_device(activations, test_matrix):
@@ -392,19 +410,21 @@
             shapes = ((7, NY, n, LANES), (3, n, LANES), (3, q, LANES))
         bufs += [pltpu.VMEM(s, F32) for s in shapes]
     block = (NY, NZ, k, LANES)
-    return pl.pallas_call(
+    hbm = pl.BlockSpec(memory_space=pl.ANY)
+    basis_t, total, inverse = pl.pallas_call(
         functools.partial(kernel, n_total),
         out_shape=(
-            jax.ShapeDtypeStruct((rows, k), F32),
-            jax.ShapeDtypeStruct((k, width), F32),
+            jax.ShapeDtypeStruct((k, rows), F32),
+            jax.ShapeDtypeStruct((NZ, k, LANES), F32),
+            jax.ShapeDtypeStruct((k, k), F32),
         ),
-        in_specs=[pl.BlockSpec(memory_space=pl.ANY)] * 2,
-        out_specs=(pl.BlockSpec(memory_space=pltpu.VMEM), pl.BlockSpec(memory_space=pltpu.VMEM)),
+        in_specs=[hbm] * 2,
+        out_specs=(hbm, hbm, hbm),
         scratch_shapes=[
             pltpu.VMEM((d // width, rows, width), BF16),
-            pltpu.VMEM((d // width, width, k), BF16),
+            pltpu.VMEM((d // width, k, width), BF16),
             pltpu.VMEM((rows, k), F32),
-            pltpu.VMEM((2 * k, rows), BF16),
+            pltpu.VMEM((k, 2 * rows), BF16),
             pltpu.VMEM(block, F32),
             pltpu.VMEM(block, F32),
             pltpu.VMEM(block, F32),
@@ -415,14 +435,34 @@
             pltpu.VMEM((NZ, 8, 384), F32),
             pltpu.VMEM((256, 384), F32),
             pltpu.VMEM((k, k), F32),
+            pltpu.VMEM((k, rows), F32),
             pltpu.SemaphoreType.DMA((2 * d // width,)),
+            pltpu.SemaphoreType.DMA((2 + len(CHUNKS),)),
             pltpu.SemaphoreType.DMA((64,)),
         ] + bufs,
         compiler_params=pltpu.CompilerParams(
             collective_id=0, has_side_effects=True, vmem_limit_bytes=56 * 1024 * 1024
         ),
         name="range_finder",
-    )(activations, test_matrix)
+    )(activations, test_matrix.T)
+    steps = NZ // 2
+    basis_t, coeffs = pl.pallas_call(
+        functools.partial(finish_kernel, n_total, steps),
+        grid=(steps,),
+        out_shape=(
+            jax.ShapeDtypeStruct((k, rows), F32),
+            jax.ShapeDtypeStruct((k, width), F32),
+        ),
+        in_specs=[
+            hbm,
+            pl.BlockSpec((2, k, LANES), lambda i: (i, 0, 0)),
+            pl.BlockSpec((k, k), lambda i: (0, 0)),
+        ],
+        out_specs=(hbm, pl.BlockSpec((k, 2 * LANES), lambda i: (0, i))),
+        scratch_shapes=[pltpu.SemaphoreType.DMA],
+        name="apply_inverse",
+    )(basis_t, total, inverse)
+    return basis_t.T, coeffs
 
 
 def solution(mesh):

time: 125 us -> 128 us (1.024)
  Pallas kernels: 111 us -> 127 us
  local copies, waits for them, and re-layouts: 12.9 us -> 0 us
    pallas_call x0 -> x1, Pallas kernels: none -> 22.8 us  [per_device(): pl.pallas_call(functools.partial(finish_kernel, n_total, steps), grid=(st...]
    unnamed x2 -> x0, local copies, waits for them, and re-layouts: 10.7 us -> none
    pallas_call x1, Pallas kernels: 111 us -> 104 us  [per_device(): pl.pallas_call(functools.partial(kernel, n_total), out_shape=(jax.ShapeDt...]
    pallas_call x1 -> x0, local copies, waits for them, and re-layouts: 2.22 us -> none  [per_device(): pl.pallas_call(functools.partial(kernel, n_total), out_shape=(jax.ShapeDt...]
where the time goes in v2:
time: 128 us
  Pallas kernels  127 us (99%)
    pallas_call x1, Pallas kernels, per_device(): pl.pallas_call(functools.partial(kernel, n_total), out_shape=(jax.ShapeDt...  104 us
    pallas_call x1, Pallas kernels, per_device(): pl.pallas_call(functools.partial(finish_kernel, n_total, steps), grid=(st...  22.8 us

profile of v2, /device:TPU:8, one launch (start us, length us, event | category | flops | bytes accessed | tf_op | source)
XLA Modules:
  0.0 127.5 jit_solution(8860052319131678928)
XLA Ops:
  0.6 103.9 %range_finder.1 = (f32[320,512]{1,0:T(8,128)}, f32[8,320,128]{2,1,0:T(8,128)}, f32[320,320]{1,0:T(8,128)}) custom-call(bf16[512,8192]{1,0:T(8,128)(2,1)} %a_hbm.1, bf16[320,8192]{1,0:T(8,128)(2,1)} %bitcast.2), custom_call_target="tpu_custom_call" | custom-call | tf_op jit(solution)/shard_map/range_finder/pallas_call | solution.py:414
  104.5 22.8 %apply_inverse.1 = (f32[320,512]{1,0:T(8,128)}, f32[320,1024]{1,0:T(8,128)}) custom-call(f32[320,512]{1,0:T(8,128)} %get-tuple-element.7.basis_hbm, f32[8,320,128]{2,1,0:T(8,128)} %get-tuple-element.8.total_ref, f32[320,320]{1,0:T(8,128)} %get-tuple-element.9.inv_ref), custom_call_target="tpu_custom_call" | custom-call | tf_op jit(solution)/shard_map/apply_inverse/pallas_call | solution.py:449

commit v3 on v2

v3 whole, which is shorter than its diff:
```python
import functools
import math

import jax
import jax.numpy as jnp
from jax import lax
from jax.experimental import pallas as pl
from jax.experimental.pallas import tpu as pltpu
from jax.sharding import PartitionSpec as P

MESH = pl.DeviceIdType.MESH
HIGHEST = lax.Precision.HIGHEST
F32 = jnp.float32
BF16 = jnp.bfloat16
NX, NY, NZ = 4, 4, 8
BLOCK = 64
LANES = 128
SEMAPHORES = 200

CHUNKS = (
    ("y", 0, 32, False),
    ("y", 32, 32, False),
    ("y", 64, 32, False),
    ("y", 96, 32, True),
    ("y", 128, 32, False),
    ("x", 160, 32, False),
    ("x", 192, 32, False),
    ("x", 224, 32, False),
    ("x", 256, 32, True),
    ("z", 288, 32, False),
)

ORDER = (
    ("owner", -1, 0), ("ya", 0, 0), ("ya", 1, 0), ("ya", 2, 0), ("ya", 3, 0), ("ya", 4, 0), ("xa", 5, 0),
    ("xa", 6, 0), ("xa", 7, 0), ("xa", 8, 0), ("za", 9, 0), ("gram_line", -1, 0), ("owner", -1, 1), ("xa", 5, 1),
    ("xa", 6, 1), ("xa", 7, 1), ("xa", 8, 1), ("za", 9, 1), ("xb", 5, 0), ("xb", 6, 0), ("owner", -1, 2),
    ("xa", 5, 2), ("xa", 6, 2), ("xa", 7, 2), ("xa", 8, 2), ("za", 9, 2), ("yb", 0, 0), ("xb", 7, 0), ("xb", 8, 0),
    ("yb", 1, 0), ("xb", 5, 1), ("xb", 6, 1), ("owner", -1, 3), ("xa", 5, 3), ("xa", 6, 3), ("xa", 7, 3),
    ("xa", 8, 3), ("za", 9, 3), ("yb", 2, 0), ("xb", 7, 1), ("xb", 8, 1), ("yb", 3, 0), ("xb", 5, 2), ("xb", 6, 2),
    ("xb", 7, 2), ("gram_spread", -1, 0), ("yb", 4, 0), ("xb", 8, 2), ("y2", 0, 0), ("xb", 5, 3), ("xb", 6, 3),
    ("xb", 7, 3), ("xb", 8, 3), ("y2", 1, 0), ("z2", 9, 0), ("y2", 2, 0), ("y3", 0, 0), ("y2", 3, 0), ("x2", 5, 0),
    ("gram_core", -1, 0), ("x2", 6, 0), ("x2", 7, 0), ("x2", 8, 0), ("gram_ready", -1, 0), ("factor", -1, 0),
    ("y3", 1, 0), ("z3", 9, 0), ("y3", 2, 0), ("c4", 0, 0), ("y2", 4, 0), ("x3", 5, 0), ("factor", -1, 1),
    ("y3", 3, 0), ("x3", 6, 0), ("factor", -1, 2), ("c4", 9, 0), ("c4", 1, 0), ("y3", 4, 0), ("x3", 7, 0),
    ("x3", 8, 0), ("c4", 2, 0), ("factor", -1, 3), ("c5", 0, 0), ("c4", 3, 0), ("c4", 5, 0), ("factor", -1, 4),
    ("c5", 9, 0), ("c4", 6, 0), ("basis", -1, 0), ("c5", 1, 0), ("c4", 4, 0), ("c4", 7, 0), ("c6", 0, 0),
    ("c5", 3, 0), ("c4", 8, 0), ("c5", 2, 0), ("c5", 5, 0), ("c6", 9, 0), ("c5", 6, 0), ("c6", 1, 0), ("c5", 8, 0),
    ("c5", 4, 0), ("c5", 7, 0), ("c6", 2, 0), ("c6", 5, 0), ("c6", 3, 0), ("c6", 6, 0), ("c6", 4, 0), ("c6", 7, 0),
    ("c6", 8, 0),
)


def inverse_factor_block(block):
    n = block.shape[0]
    rows = lax.broadcasted_iota(jnp.int32, (n, n), 0)
    cols = lax.broadcasted_iota(jnp.int32, (n, n), 1)
    state = jnp.concatenate([block, jnp.where(rows == cols, 1.0, 0.0).astype(F32)], axis=1)
    row_in_group = lax.broadcasted_iota(jnp.int32, (8, 2 * n), 0)
    done = []
    for group in range(n // 8):
        left = n - 8 * group
        head = state[0:8, :]
        columns = [
            jnp.broadcast_to(state[:, 8 * group + j : 8 * group + j + 1], (left, 2 * n))
            for j in range(8)
        ]
        pivot_rows, pivot_cols = [], []
        for j in range(8):
            inv = lax.rsqrt(columns[j][j : j + 1, :])
            row = head[j : j + 1, :] * inv
            col = columns[j] * inv
            pivot_rows.append(row)
            pivot_cols.append(col)
            if j < 7:
                head = head - col[0:8] * row
            for later in range(j + 1, 8):
                columns[later] = columns[later] - col * col[later : later + 1, :]
        out = jnp.broadcast_to(pivot_rows[0], (8, 2 * n))
        for j in range(1, 8):
            out = jnp.where(row_in_group == j, pivot_rows[j], out)
        done.append(out)
        if left > 8:
            state = state[8:, :]
            for j in range(8):
                state = state - pivot_cols[j][8:] * pivot_rows[j]
    return jnp.concatenate(done, axis=0)[:, n:]


def factor_step(m_ref, step):
    k = m_ref.shape[0]
    lo, hi = step * BLOCK, (step + 1) * BLOCK
    inverse = inverse_factor_block(m_ref[lo:hi, lo:hi])
    rows = lax.broadcasted_iota(jnp.int32, (BLOCK, BLOCK), 0)
    cols = lax.broadcasted_iota(jnp.int32, (BLOCK, BLOCK), 1)
    m_ref[lo:hi, lo:hi] = jnp.where(rows == cols, 1.0, 0.0).astype(F32)
    panel = jnp.dot(inverse, m_ref[lo:hi, :], precision=HIGHEST, preferred_element_type=F32)
    m_ref[lo:hi, :] = panel
    if hi < k:
        m_ref[hi:, lo:hi] = jnp.zeros((k - hi, BLOCK), F32)
        m_ref[hi:, :] -= lax.dot_general(
            panel[:, hi:], panel, (((0,), (0,)), ((), ())),
            precision=HIGHEST, preferred_element_type=F32,
        )


def kernel(n_total, a_hbm, om_hbm, basis_hbm, total_hbm, inv_hbm,
           a_buf, om_buf, sketch, halves, to_core, from_core, part, total,
           folded, g_core, g_plane, g_line, g_sum, mat, basis_t, load_sem, out_sem, sems, *flat_bufs):
    rows_here, k = sketch.shape
    bufs = [flat_bufs[4 * i : 4 * i + 4] for i in range(len(CHUNKS))]
    wide, narrow = lax.axis_index("wide"), lax.axis_index("narrow")
    x, z = lax.rem(wide, NX), wide // NX
    y, c = narrow // 2, lax.rem(narrow, 2)

    def device(xx, yy, zz, cc):
        return (zz * NX + xx, yy * 2 + cc)

    sibling = device(x, y, z, 1 - c)
    on_x = [(lax.rem(x + d, NX), device(lax.rem(x + d, NX), y, z, c)) for d in range(1, NX)]
    on_y = [(lax.rem(y + d, NY), device(x, lax.rem(y + d, NY), z, c)) for d in range(1, NY)]
    on_z = [(lax.rem(z + d, NZ), device(x, y, lax.rem(z + d, NZ), c)) for d in range(1, NZ)]
    place = y * NX + x
    on_plane = []
    for d in range(1, NX * NY):
        other = lax.rem(place + d, NX * NY)
        on_plane.append((other, device(lax.rem(other, NX), other // NX, z, c)))

    used = [0]
    pending = []

    def exchange(size_like):
        at = used[0]
        used[0] += 2
        pending.append((at, size_like))
        return at

    def send(at, src, dst, to):
        pltpu.make_async_remote_copy(
            src_ref=src, dst_ref=dst, send_sem=sems.at[at], recv_sem=sems.at[at + 1],
            device_id=to, device_id_type=MESH,
        ).start()

    def wait_bytes(sem, like):
        pltpu.make_async_copy(like, like, sem).wait()

    def received(at, like):
        wait_bytes(sems.at[at + 1], like)

    barrier = pltpu.get_barrier_semaphore()
    partners = [sibling] + [to for _, to in on_plane] + [to for _, to in on_z]
    n_blocks, _, width = a_buf.shape
    loads = []
    for j in range(n_blocks):
        loads.append((
            pltpu.make_async_copy(a_hbm.at[:, pl.ds(j * width, width)], a_buf.at[j], load_sem.at[j]),
            pltpu.make_async_copy(om_hbm.at[:, pl.ds(j * width, width)], om_buf.at[j], load_sem.at[n_blocks + j]),
        ))
    for first, second in loads:
        first.start()
        second.start()
    for to in partners:
        pl.semaphore_signal(barrier, inc=1, device_id=to, device_id_type=MESH)

    for j in range(n_blocks):
        loads[j][0].wait()
        loads[j][1].wait()
        term = lax.dot_general(
            a_buf[j], om_buf[j], (((1,), (1,)), ((), ())), preferred_element_type=F32
        )
        if j == 0:
            sketch[...] = term
        else:
            sketch[...] += term

    value = sketch[...]
    high = value.astype(BF16)
    low = (value - high.astype(F32)).astype(BF16)
    halves[:, 0:rows_here] = high.T
    halves[:, rows_here:] = low.T

    def project(block, dst, at):
        cols = a_buf[block]
        res = jnp.dot(
            halves[...], jnp.concatenate([cols, cols], axis=0), preferred_element_type=F32
        )
        for t in range(NZ):
            dst[at, t] = res[:, t * LANES : (t + 1) * LANES]

    owners = [lax.rem(y + d, NY) for d in (2, 1, 3, 0)]
    ex_owner = []

    def to_sibling(o):
        project(2 * o + 1 - c, to_core, o)
        at = exchange(from_core.at[o])
        ex_owner.append(at)
        send(at, to_core.at[o], from_core.at[o], sibling)

    pl.semaphore_wait(barrier, len(partners))
    to_sibling(owners[0])

    gram = lax.dot_general(
        sketch[...], sketch[...], (((0,), (0,)), ((), ())),
        precision=HIGHEST, preferred_element_type=F32,
    )
    folded[...] = jnp.zeros(folded.shape, F32)
    folded[0:128, 0:k] = gram[0:128, :]
    folded[128:256, 0 : k - 128] = gram[128:256, 128:]
    folded[128 : k - 128, 256 : k] = gram[256:, 256:]
    half_rows = g_core.shape[0]
    mine = pl.multiple_of(c * half_rows, 8)
    yours = pl.multiple_of((1 - c) * half_rows, 8)
    ex_core = exchange(g_core)
    send(ex_core, folded.at[pl.ds(yours, half_rows)], g_core, sibling)

    for o in owners[1:]:
        to_sibling(o)
    received(ex_core, g_core)
    folded[pl.ds(mine, half_rows)] += g_core[...]
    my_tile = pl.multiple_of(c * half_rows + place * 8, 8)
    ex_plane = exchange(g_plane)
    for d, (other, to) in enumerate(on_plane):
        src = folded.at[pl.ds(pl.multiple_of(c * half_rows + other * 8, 8), 8)]
        send(ex_plane, src, g_plane.at[d], to)

    half = NZ // 2

    def rows_of(ch):
        return pl.ds(CHUNKS[ch][1], CHUNKS[ch][2])

    def quarter(ch, d):
        q = CHUNKS[ch][2] // NX
        return pl.ds(pl.multiple_of(CHUNKS[ch][1] + lax.rem(x + d, NX) * q, 8), q)

    flying = {}

    def began(name, ch, like, i=0):
        at = exchange(like)
        flying[name, ch, i] = (at, like)
        return at

    def arrived(name, ch, i=0):
        received(*flying[name, ch, i])

    def summed(buf, n):
        acc = buf[0]
        for d in range(1, n):
            acc = acc + buf[d]
        return acc

    def owner(ch, i):
        o = owners[i]
        project(2 * o + c, part, o)
        received(ex_owner[i], from_core.at[o])

        def add(t, carry):
            part[o, t] += from_core[o, t]
            return carry

        lax.fori_loop(0, NZ, add, 0)

    def ya(ch, i):
        buf, rows = bufs[ch][0], rows_of(ch)
        at = began("a", ch, buf)
        send(at, part.at[owners[0], 0:half, rows, :], buf.at[0], on_y[0][1])
        send(at, part.at[owners[0], half:NZ, rows, :], buf.at[1], on_y[2][1])

    def yb(ch, i):
        arrived("a", ch)
        old, buf, rows = bufs[ch][0], bufs[ch][1], rows_of(ch)
        part[owners[1], 0:half, rows, :] += old[0]
        part[owners[2], half:NZ, rows, :] += old[1]
        at = began("b", ch, buf)
        send(at, part.at[owners[1], :, rows, :], buf.at[0], on_y[0][1])
        send(at, part.at[owners[2], :, rows, :], buf.at[1], on_y[2][1])

    def y2(ch, i):
        arrived("b", ch)
        old, buf, rows = bufs[ch][1], bufs[ch][2], rows_of(ch)
        part[y, :, rows, :] += old[0] + old[1]
        at = began("2", ch, buf)
        for d in range(1, NX):
            send(at, part.at[y, :, quarter(ch, d), :], buf.at[d - 1], on_x[d - 1][1])

    def y3(ch, i):
        arrived("2", ch)
        old, buf, rows = bufs[ch][2], bufs[ch][3], quarter(ch, 0)
        part[y, :, rows, :] += summed(old, 3)
        at = began("3", ch, buf)
        for d, (zz, to) in enumerate(on_z):
            send(at, part.at[y, zz, rows, :], buf.at[d], to)

    def xa(ch, i):
        buf, rows = bufs[ch][0], quarter(ch, 2)
        at = began("a", ch, buf.at[i], i)
        send(at, part.at[owners[i], 0:half, rows, :], buf.at[i, 0], on_x[0][1])
        send(at, part.at[owners[i], half:NZ, rows, :], buf.at[i, 1], on_x[2][1])

    def xb(ch, i):
        arrived("a", ch, i)
        old, buf = bufs[ch][0], bufs[ch][1]
        up, down = quarter(ch, 1), quarter(ch, 3)
        part[owners[i], 0:half, up, :] += old[i, 0]
        part[owners[i], half:NZ, down, :] += old[i, 1]
        at = began("b", ch, buf.at[i], i)
        send(at, part.at[owners[i], :, up, :], buf.at[i, 0], on_x[0][1])
        send(at, part.at[owners[i], :, down, :], buf.at[i, 1], on_x[2][1])

    def x2(ch, i):
        old, buf, rows = bufs[ch][1], bufs[ch][2], quarter(ch, 0)
        for j in range(NY):
            arrived("b", ch, j)
            part[owners[j], :, rows, :] += old[j, 0] + old[j, 1]
        at = began("2", ch, buf)
        for d, (yy, to) in enumerate(on_y):
            send(at, part.at[yy, :, rows, :], buf.at[d], to)

    x3 = y3

    def za(ch, i):
        buf, rows = bufs[ch][0], rows_of(ch)
        at = began("a", ch, buf.at[i], i)
        for d, (zz, to) in enumerate(on_z):
            send(at, part.at[owners[i], zz, rows, :], buf.at[i, d], to)

    def z2(ch, i):
        old, buf, rows = bufs[ch][0], bufs[ch][2], rows_of(ch)
        for j in range(NY):
            arrived("a", ch, j)
            part[owners[j], z, rows, :] += summed(old.at[j], NZ - 1)
        at = began("2", ch, buf)
        for d, (yy, to) in enumerate(on_y):
            send(at, part.at[yy, z, rows, :], buf.at[d], to)

    def z3(ch, i):
        arrived("2", ch)
        old, buf, rows = bufs[ch][2], bufs[ch][3], rows_of(ch)
        part[y, z, rows, :] += summed(old, 3)
        at = began("3", ch, buf)
        for d in range(1, NX):
            send(at, part.at[y, z, quarter(ch, d), :], buf.at[d - 1], on_x[d - 1][1])

    def c4(ch, i):
        arrived("3", ch)
        old, rows, q = bufs[ch][3], quarter(ch, 0), CHUNKS[ch][2] // NX
        total[z, rows, :] = part[y, z, rows, :] + summed(old, old.shape[0])
        line = on_x if CHUNKS[ch][3] else on_z
        at = began("4", ch, total.at[0 : len(line), 0:q, :])
        for _, to in line:
            send(at, total.at[z, rows, :], total.at[z, rows, :], to)

    def c5(ch, i):
        arrived("4", ch)
        n = CHUNKS[ch][2]
        if CHUNKS[ch][3]:
            at = began("5", ch, total.at[0 : NZ - 1, 0:n, :])
            for _, to in on_z:
                send(at, total.at[z, rows_of(ch), :], total.at[z, rows_of(ch), :], to)
        else:
            at = began("5", ch, total.at[:, 0 : 3 * n // NX, :])
            for _, to in on_x:
                send(at, total.at[:, quarter(ch, 0), :], total.at[:, quarter(ch, 0), :], to)

    outs = []

    def c6(ch, i):
        arrived("5", ch)
        copy = pltpu.make_async_copy(
            total.at[:, rows_of(ch), :], total_hbm.at[:, rows_of(ch), :], out_sem.at[2 + ch]
        )
        copy.start()
        outs.append(copy)

    tile = pl.ds(my_tile, 8)

    def gram_line(ch, i):
        received(ex_plane, g_plane)
        g_line[z] = folded[tile, :] + summed(g_plane, NX * NY - 1)
        at = began("g", -1, g_plane.at[0 : NZ - 1])
        for _, to in on_z:
            send(at, g_line.at[z], g_line.at[z], to)

    def gram_spread(ch, i):
        arrived("g", -1)
        g_sum[tile, :] = summed(g_line, NZ)
        at = began("h", -1, g_plane)
        for _, to in on_plane:
            send(at, g_sum.at[tile], g_sum.at[tile], to)

    def gram_core(ch, i):
        arrived("h", -1)
        at = began("i", -1, g_core)
        my_half = pl.ds(mine, half_rows)
        send(at, g_sum.at[my_half], g_sum.at[my_half], sibling)

    def gram_ready(ch, i):
        arrived("i", -1)
        mat[0:128, :] = g_sum[0:128, 0:k]
        mat[128:256, 128:] = g_sum[128:256, 0 : k - 128]
        mat[256:, 256:] = g_sum[128 : k - 128, 256 : k]

    def factor(ch, i):
        factor_step(mat, i)

    def basis(ch, i):
        rows = lax.broadcasted_iota(jnp.int32, (k, k), 0)
        cols = lax.broadcasted_iota(jnp.int32, (k, k), 1)
        mat[...] = jnp.where(rows >= cols, mat[...], 0.0)
        basis_t[...] = lax.dot_general(
            mat[...], sketch[...], (((1,), (1,)), ((), ())),
            precision=HIGHEST, preferred_element_type=F32,
        ) * math.sqrt(n_total)
        for j, (src, dst) in enumerate(((mat, inv_hbm), (basis_t, basis_hbm))):
            copy = pltpu.make_async_copy(src, dst, out_sem.at[j])
            copy.start()
            outs.append(copy)

    steps = dict(
        owner=owner, ya=ya, yb=yb, y2=y2, y3=y3, xa=xa, xb=xb, x2=x2, x3=x3, za=za, z2=z2, z3=z3,
        c4=c4, c5=c5, c6=c6, gram_line=gram_line, gram_spread=gram_spread, gram_core=gram_core,
        gram_ready=gram_ready, factor=factor, basis=basis,
    )
    for name, ch, i in ORDER:
        steps[name](ch, i)
    for copy in outs:
        copy.wait()
    for at, like in pending:
        wait_bytes(sems.at[at], like)


def finish_kernel(n_total, basis_in, total_ref, inv_ref, basis_out, coef_ref):
    basis_out[...] = basis_in[...]
    both = jnp.concatenate([total_ref[0], total_ref[1]], axis=1)
    coef_ref[...] = jnp.dot(
        inv_ref[...], both, precision=HIGHEST, preferred_element_type=F32
    ) * (1.0 / math.sqrt(n_total))


def per_device(activations, test_matrix):
    rows, d = activations.shape
    k = test_matrix.shape[1]
    n_total = rows * lax.axis_size("wide") * lax.axis_size("narrow")
    width = d // (2 * NY)
    bufs = []
    half = NZ // 2
    for axis, _, n, _ in CHUNKS:
        q = n // NX
        if axis == "y":
            shapes = ((2, half, n, LANES), (2, NZ, n, LANES), (3, NZ, q, LANES), (7, q, LANES))
        elif axis == "x":
            shapes = (
                (NY, 2, half, q, LANES), (NY, 2, NZ, q, LANES), (3, NZ, q, LANES), (7, q, LANES)
            )
        else:
            shapes = ((NY, 7, n, LANES), (8, LANES), (3, n, LANES), (3, q, LANES))
        bufs += [pltpu.VMEM(s, F32) for s in shapes]
    block = (NY, NZ, k, LANES)
    hbm = pl.BlockSpec(memory_space=pl.ANY)
    basis_t, total, inverse = pl.pallas_call(
        functools.partial(kernel, n_total),
        out_shape=(
            jax.ShapeDtypeStruct((k, rows), F32),
            jax.ShapeDtypeStruct((NZ, k, LANES), F32),
            jax.ShapeDtypeStruct((k, k), F32),
        ),
        in_specs=[hbm] * 2,
        out_specs=(hbm, hbm, hbm),
        scratch_shapes=[
            pltpu.VMEM((d // width, rows, width), BF16),
            pltpu.VMEM((d // width, k, width), BF16),
            pltpu.VMEM((rows, k), F32),
            pltpu.VMEM((k, 2 * rows), BF16),
            pltpu.VMEM(block, F32),
            pltpu.VMEM(block, F32),
            pltpu.VMEM(block, F32),
            pltpu.VMEM((NZ, k, LANES), F32),
            pltpu.VMEM((256, 384), F32),
            pltpu.VMEM((128, 384), F32),
            pltpu.VMEM((NX * NY - 1, 8, 384), F32),
            pltpu.VMEM((NZ, 8, 384), F32),
            pltpu.VMEM((256, 384), F32),
            pltpu.VMEM((k, k), F32),
            pltpu.VMEM((k, rows), F32),
            pltpu.SemaphoreType.DMA((2 * d // width,)),
            pltpu.SemaphoreType.DMA((2 + len(CHUNKS),)),
            pltpu.SemaphoreType.DMA((SEMAPHORES,)),
        ] + bufs,
        compiler_params=pltpu.CompilerParams(
            collective_id=0, has_side_effects=True, vmem_limit_bytes=56 * 1024 * 1024
        ),
        name="range_finder",
    )(activations, test_matrix.T)
    steps = NZ // 2
    by_columns = pl.BlockSpec((k, rows // steps), lambda i: (0, i))
    basis_t, coeffs = pl.pallas_call(
        functools.partial(finish_kernel, n_total),
        grid=(steps,),
        out_shape=(
            jax.ShapeDtypeStruct((k, rows), F32),
            jax.ShapeDtypeStruct((k, width), F32),
        ),
        in_specs=[
            by_columns,
            pl.BlockSpec((2, k, LANES), lambda i: (i, 0, 0)),
            pl.BlockSpec((k, k), lambda i: (0, 0)),
        ],
        out_specs=(by_columns, pl.BlockSpec((k, 2 * LANES), lambda i: (0, i))),
        name="apply_inverse",
    )(basis_t, total, inverse)
    return basis_t.T, coeffs


def solution(mesh):
    return jax.shard_map(
        per_device,
        mesh=mesh,
        in_specs=(P(("wide", "narrow"), None), P()),
        out_specs=(P(("wide", "narrow"), None), P(None, "narrow")),
        check_vma=False,
    )
```

time: 128 us -> 82.2 us (0.64)
  Pallas kernels: 127 us -> 80.5 us
    pallas_call x1, Pallas kernels: 104 us -> 75.1 us  [per_device(): pl.pallas_call(functools.partial(kernel, n_total), out_shape=(jax.ShapeDt...]
    pallas_call x1, Pallas kernels: 22.8 us -> 5.32 us  [per_device(): pl.pallas_call(functools.partial(finish_kernel, n_total), grid=(steps,),...]
where the time goes in v3:
time: 82.2 us; the launch traced here: 81.1 us
  Pallas kernels  80.5 us (98%)
    pallas_call x1, Pallas kernels, per_device(): pl.pallas_call(functools.partial(kernel, n_total), out_shape=(jax.ShapeDt...  75.1 us
    pallas_call x1, Pallas kernels, per_device(): pl.pallas_call(functools.partial(finish_kernel, n_total), grid=(steps,),...  5.32 us

profile of v3, /device:TPU:8, one launch (start us, length us, event | category | flops | bytes accessed | tf_op | source)
XLA Modules:
  0.0 81.1 jit_solution(1022561543885925742)
XLA Ops:
  0.6 75.1 %range_finder.1 = (f32[320,512]{1,0:T(8,128)}, f32[8,320,128]{2,1,0:T(8,128)}, f32[320,320]{1,0:T(8,128)}) custom-call(bf16[512,8192]{1,0:T(8,128)(2,1)} %a_hbm.1, bf16[320,8192]{1,0:T(8,128)(2,1)} %bitcast.2), custom_call_target="tpu_custom_call" | custom-call | tf_op jit(solution)/shard_map/range_finder/pallas_call | solution.py:458
  75.8 5.3 %apply_inverse.1 = (f32[320,512]{1,0:T(8,128)}, f32[320,1024]{1,0:T(8,128)}) custom-call(f32[320,512]{1,0:T(8,128)} %get-tuple-element.7.basis_in, f32[8,320,128]{2,1,0:T(8,128)} %get-tuple-element.8.total_ref, f32[320,320]{1,0:T(8,128)} %get-tuple-element.9.inv_ref), custom_call_target="tpu_custom_call" | custom-call | tf_op jit(solution)/shard_map/apply_inverse/pallas_call | solution.py:494

commit v4 on v3

v4 whole, which is shorter than its diff:
```python
import functools
import math

import jax
import jax.numpy as jnp
from jax import lax
from jax.experimental import pallas as pl
from jax.experimental.pallas import tpu as pltpu
from jax.sharding import PartitionSpec as P

MESH = pl.DeviceIdType.MESH
HIGHEST = lax.Precision.HIGHEST
F32 = jnp.float32
BF16 = jnp.bfloat16
NX, NY, NZ = 4, 4, 8
BLOCK = 64
LANES = 128
SEMAPHORES = 176
BEFORE_GRAM = 3

CHUNKS = (
    ("y", 0, 32, True),
    ("x", 32, 32, False),
    ("x", 64, 32, False),
    ("y", 96, 32, False),
    ("y", 128, 32, True),
    ("x", 160, 32, False),
    ("z", 192, 32, False),
    ("x", 224, 32, False),
    ("z", 256, 32, False),
    ("y", 288, 32, True),
)

ORDER = (
    ("ya", 0), ("xa", 1), ("xa", 2), ("gram_plane", -1), ("ya", 3), ("ya", 4), ("xa", 5), ("yb", 0),
    ("xb", 1), ("za", 6), ("xa", 7), ("xb", 2), ("za", 8), ("yb", 3), ("gram_line", -1), ("ya", 9), ("yb", 4),
    ("xb", 5), ("y2", 0), ("zb", 6), ("x2", 1), ("xb", 7), ("y2", 3), ("zb", 8), ("yb", 9), ("x2", 2),
    ("gram_spread", -1), ("y2", 4), ("x2", 5), ("y3", 1), ("y3", 0), ("z2", 6), ("y2", 9), ("x2", 7),
    ("y3", 2), ("y3", 3), ("z2", 8), ("gram_core", -1), ("y3", 5), ("y3", 4), ("z3", 6), ("c4", 1), ("c4", 0),
    ("gram_ready", -1), ("y3", 7), ("y3", 9), ("factor", 0), ("c4", 2), ("z3", 8), ("factor", 1), ("c4", 3),
    ("c4", 6), ("factor", 2), ("c4", 5), ("c5", 0), ("c4", 4), ("factor", 3), ("c5", 1), ("c4", 7), ("c4", 8),
    ("factor", 4), ("c4", 9), ("c5", 2), ("factor", 5), ("c5", 3), ("c5", 4), ("c5", 6), ("factor", 6),
    ("c5", 5), ("factor", 7), ("c6", 1), ("c5", 9), ("factor", 8), ("factor", 9), ("c5", 7), ("c6", 0),
    ("c6", 2), ("factor", 10), ("c6", 3), ("c5", 8), ("factor", 11), ("c6", 6), ("factor", 12),
    ("factor", 13), ("c6", 5), ("c6", 4), ("factor", 14), ("basis", -1), ("c6", 7), ("c6", 9), ("c6", 8),
)


def eliminate(state, first, last):
    width = state.shape[1]
    row_in_group = lax.broadcasted_iota(jnp.int32, (8, width), 0)
    done = []
    for group in range(first, last):
        left = state.shape[0]
        head = state[0:8, :]
        columns = [
            jnp.broadcast_to(state[:, 8 * group + j : 8 * group + j + 1], (left, width))
            for j in range(8)
        ]
        pivot_rows, pivot_cols = [], []
        for j in range(8):
            inv = lax.rsqrt(columns[j][j : j + 1, :])
            row = head[j : j + 1, :] * inv
            col = columns[j] * inv
            pivot_rows.append(row)
            pivot_cols.append(col)
            if j < 7:
                head = head - col[0:8] * row
            for later in range(j + 1, 8):
                columns[later] = columns[later] - col * col[later : later + 1, :]
        out = jnp.broadcast_to(pivot_rows[0], (8, width))
        for j in range(1, 8):
            out = jnp.where(row_in_group == j, pivot_rows[j], out)
        done.append(out)
        if left > 8:
            state = state[8:, :]
            for j in range(8):
                state = state - pivot_cols[j][8:] * pivot_rows[j]
    return jnp.concatenate(done, axis=0), state


def factor_step(m_ref, block_ref, step, phase):
    k = m_ref.shape[0]
    lo, hi = step * BLOCK, (step + 1) * BLOCK
    half, groups = BLOCK // 2, BLOCK // 8
    rows = lax.broadcasted_iota(jnp.int32, (BLOCK, BLOCK), 0)
    cols = lax.broadcasted_iota(jnp.int32, (BLOCK, BLOCK), 1)
    identity = jnp.where(rows == cols, 1.0, 0.0).astype(F32)
    if phase == 0:
        state = jnp.concatenate([m_ref[lo:hi, lo:hi], identity], axis=1)
        block_ref[0:half, :], block_ref[half:, :] = eliminate(state, 0, groups // 2)
    elif phase == 1:
        done, _ = eliminate(block_ref[half:, :], groups // 2, groups)
        inverse = jnp.concatenate([block_ref[0:half, BLOCK:], done[:, BLOCK:]], axis=0)
        m_ref[lo:hi, lo:hi] = identity
        m_ref[lo:hi, :] = jnp.dot(
            inverse, m_ref[lo:hi, :], precision=HIGHEST, preferred_element_type=F32
        )
    elif hi < k:
        panel = m_ref[lo:hi, :]
        m_ref[hi:, lo:hi] = jnp.zeros((k - hi, BLOCK), F32)
        m_ref[hi:, :] -= lax.dot_general(
            panel[:, hi:], panel, (((0,), (0,)), ((), ())),
            precision=HIGHEST, preferred_element_type=F32,
        )


def kernel(n_total, a_hbm, om_hbm, basis_hbm, total_hbm, inv_hbm,
           a_buf, om_buf, sketch, halves, to_core, from_core, part, total,
           folded, g_core, g_plane, g_line, g_sum, mat, block, basis_t, load_sem, out_sem, sems, *flat_bufs):
    k, rows_here = sketch.shape
    bufs = [flat_bufs[4 * i : 4 * i + 4] for i in range(len(CHUNKS))]
    wide, narrow = lax.axis_index("wide"), lax.axis_index("narrow")
    x, z = lax.rem(wide, NX), wide // NX
    y, c = narrow // 2, lax.rem(narrow, 2)

    def device(xx, yy, zz, cc):
        return (zz * NX + xx, yy * 2 + cc)

    sibling = device(x, y, z, 1 - c)
    on_x = [(lax.rem(x + d, NX), device(lax.rem(x + d, NX), y, z, c)) for d in range(1, NX)]
    on_y = [(lax.rem(y + d, NY), device(x, lax.rem(y + d, NY), z, c)) for d in range(1, NY)]
    on_z = [(lax.rem(z + d, NZ), device(x, y, lax.rem(z + d, NZ), c)) for d in range(1, NZ)]
    place = y * NX + x
    on_plane = []
    for d in range(1, NX * NY):
        other = lax.rem(place + d, NX * NY)
        on_plane.append((other, device(lax.rem(other, NX), other // NX, z, c)))

    used = [0]
    pending = []

    def exchange(size_like):
        at = used[0]
        used[0] += 2
        pending.append((at, size_like))
        return at

    def send(at, src, dst, to):
        pltpu.make_async_remote_copy(
            src_ref=src, dst_ref=dst, send_sem=sems.at[at], recv_sem=sems.at[at + 1],
            device_id=to, device_id_type=MESH,
        ).start()

    def wait_bytes(sem, like):
        pltpu.make_async_copy(like, like, sem).wait()

    def received(at, like):
        wait_bytes(sems.at[at + 1], like)

    barrier = pltpu.get_barrier_semaphore()
    partners = [sibling] + [to for _, to in on_plane] + [to for _, to in on_z]
    n_blocks, _, width = a_buf.shape
    loads = []
    for j in range(n_blocks):
        loads.append((
            pltpu.make_async_copy(a_hbm.at[:, pl.ds(j * width, width)], a_buf.at[j], load_sem.at[j]),
            pltpu.make_async_copy(om_hbm.at[:, pl.ds(j * width, width)], om_buf.at[j], load_sem.at[n_blocks + j]),
        ))
    for first, second in loads:
        first.start()
        second.start()
    for to in partners:
        pl.semaphore_signal(barrier, inc=1, device_id=to, device_id_type=MESH)

    for j in range(n_blocks):
        loads[j][0].wait()
        loads[j][1].wait()
        term = lax.dot_general(
            om_buf[j], a_buf[j], (((1,), (1,)), ((), ())), preferred_element_type=F32
        )
        if j == 0:
            sketch[...] = term
        else:
            sketch[...] += term

    value = sketch[...]
    high = value.astype(BF16)
    low = (value - high.astype(F32)).astype(BF16)
    halves[:, 0:rows_here] = high
    halves[:, rows_here:] = low

    def project(block, dst, at):
        cols = a_buf[block]
        res = jnp.dot(
            halves[...], jnp.concatenate([cols, cols], axis=0), preferred_element_type=F32
        )
        for t in range(NZ):
            dst[at, t] = res[:, t * LANES : (t + 1) * LANES]

    pl.semaphore_wait(barrier, len(partners))
    for o in range(NY):
        project(2 * o + 1 - c, to_core, o)
    ex_chunk = []

    def to_sibling(chunks):
        for _, first, n, _ in chunks:
            rows = pl.ds(first, n)
            at = exchange(from_core.at[:, :, rows, :])
            ex_chunk.append(at)
            send(at, to_core.at[:, :, rows, :], from_core.at[:, :, rows, :], sibling)

    to_sibling(CHUNKS[:BEFORE_GRAM])

    gram = lax.dot_general(
        sketch[...], sketch[...], (((1,), (1,)), ((), ())),
        precision=HIGHEST, preferred_element_type=F32,
    )
    folded[...] = jnp.zeros(folded.shape, F32)
    folded[0:128, 0:k] = gram[0:128, :]
    folded[128:256, 0 : k - 128] = gram[128:256, 128:]
    folded[128 : k - 128, 256 : k] = gram[256:, 256:]
    half_rows = g_core.shape[0]
    mine = pl.multiple_of(c * half_rows, 8)
    yours = pl.multiple_of((1 - c) * half_rows, 8)
    ex_core = exchange(g_core)
    send(ex_core, folded.at[pl.ds(yours, half_rows)], g_core, sibling)
    to_sibling(CHUNKS[BEFORE_GRAM:])
    for o in range(NY):
        project(2 * o + c, part, o)

    my_tile = pl.multiple_of(c * half_rows + place * 8, 8)

    half = NZ // 2

    def rows_of(ch):
        return pl.ds(CHUNKS[ch][1], CHUNKS[ch][2])

    def quarter(ch, d):
        q = CHUNKS[ch][2] // NX
        return pl.ds(pl.multiple_of(CHUNKS[ch][1] + lax.rem(x + d, NX) * q, 8), q)

    flying = {}

    def began(name, ch, like):
        at = exchange(like)
        flying[name, ch] = (at, like)
        return at

    def arrived(name, ch):
        received(*flying[name, ch])

    def summed(buf, n):
        acc = buf[0]
        for d in range(1, n):
            acc = acc + buf[d]
        return acc

    def from_sibling(ch):
        rows = rows_of(ch)
        received(ex_chunk[ch], from_core.at[:, :, rows, :])

        def add(o, carry):
            part[o, :, rows, :] += from_core[o, :, rows, :]
            return carry

        lax.fori_loop(0, NY, add, 0)

    far, up_y, down_y = [lax.rem(y + d, NY) for d in (2, 1, 3)]

    def ya(ch):
        from_sibling(ch)
        buf, rows = bufs[ch][0], rows_of(ch)
        at = began("a", ch, buf)
        send(at, part.at[far, 0:half, rows, :], buf.at[0], on_y[0][1])
        send(at, part.at[far, half:NZ, rows, :], buf.at[1], on_y[2][1])

    def yb(ch):
        arrived("a", ch)
        old, buf, rows = bufs[ch][0], bufs[ch][1], rows_of(ch)
        part[up_y, 0:half, rows, :] += old[0]
        part[down_y, half:NZ, rows, :] += old[1]
        at = began("b", ch, buf)
        send(at, part.at[up_y, :, rows, :], buf.at[0], on_y[0][1])
        send(at, part.at[down_y, :, rows, :], buf.at[1], on_y[2][1])

    def y2(ch):
        arrived("b", ch)
        old, buf, rows = bufs[ch][1], bufs[ch][2], rows_of(ch)
        part[y, :, rows, :] += old[0] + old[1]
        at = began("2", ch, buf)
        for d in range(1, NX):
            send(at, part.at[y, :, quarter(ch, d), :], buf.at[d - 1], on_x[d - 1][1])

    def y3(ch):
        arrived("2", ch)
        old, buf, rows = bufs[ch][2], bufs[ch][3], quarter(ch, 0)
        part[y, :, rows, :] += summed(old, 3)
        at = began("3", ch, buf)
        for d, (zz, to) in enumerate(on_z):
            send(at, part.at[y, zz, rows, :], buf.at[d], to)

    def xa(ch):
        from_sibling(ch)
        buf, rows = bufs[ch][0], quarter(ch, 2)
        at = began("a", ch, buf)
        send(at, part.at[:, 0:half, rows, :], buf.at[0], on_x[0][1])
        send(at, part.at[:, half:NZ, rows, :], buf.at[1], on_x[2][1])

    def xb(ch):
        arrived("a", ch)
        old, buf = bufs[ch][0], bufs[ch][1]
        up, down = quarter(ch, 1), quarter(ch, 3)
        part[:, 0:half, up, :] += old[0]
        part[:, half:NZ, down, :] += old[1]
        at = began("b", ch, buf)
        send(at, part.at[:, :, up, :], buf.at[0], on_x[0][1])
        send(at, part.at[:, :, down, :], buf.at[1], on_x[2][1])

    def x2(ch):
        arrived("b", ch)
        old, buf, rows = bufs[ch][1], bufs[ch][2], quarter(ch, 0)
        part[:, :, rows, :] += old[0] + old[1]
        at = began("2", ch, buf)
        for d, (yy, to) in enumerate(on_y):
            send(at, part.at[yy, :, rows, :], buf.at[d], to)

    def away(d):
        return lax.rem(z + d, NZ), on_z[d - 1][1]

    def za(ch):
        from_sibling(ch)
        buf, rows = bufs[ch][0], rows_of(ch)
        at = began("a", ch, buf)
        send(at, part.at[:, away(5)[0], rows, :], buf.at[0], away(7)[1])
        send(at, part.at[:, away(3)[0], rows, :], buf.at[1], away(1)[1])
        send(at, part.at[0:2, away(4)[0], rows, :], buf.at[2, 0:2], away(2)[1])
        send(at, part.at[2:NY, away(4)[0], rows, :], buf.at[2, 2:NY], away(6)[1])

    def zb(ch):
        arrived("a", ch)
        old, buf, rows = bufs[ch][0], bufs[ch][1], rows_of(ch)
        down, up = away(6)[0], away(2)[0]
        part[:, down, rows, :] += old[0]
        part[2:NY, down, rows, :] += old[2, 2:NY]
        part[:, up, rows, :] += old[1]
        part[0:2, up, rows, :] += old[2, 0:2]
        at = began("b", ch, buf)
        for slot, d in enumerate((1, 7, 2, 6)):
            zz, to = away(d)
            send(at, part.at[:, zz, rows, :], buf.at[slot], to)

    def z2(ch):
        arrived("b", ch)
        old, buf, rows = bufs[ch][1], bufs[ch][2], rows_of(ch)
        part[:, z, rows, :] += summed(old, 4)
        at = began("2", ch, buf)
        for d, (yy, to) in enumerate(on_y):
            send(at, part.at[yy, z, rows, :], buf.at[d], to)

    def z3(ch):
        arrived("2", ch)
        old, buf, rows = bufs[ch][2], bufs[ch][3], rows_of(ch)
        part[y, z, rows, :] += summed(old, 3)
        at = began("3", ch, buf)
        for d in range(1, NX):
            send(at, part.at[y, z, quarter(ch, d), :], buf.at[d - 1], on_x[d - 1][1])

    def c4(ch):
        arrived("3", ch)
        old, rows, q = bufs[ch][3], quarter(ch, 0), CHUNKS[ch][2] // NX
        total[z, rows, :] = part[y, z, rows, :] + summed(old, old.shape[0])
        line = on_x if CHUNKS[ch][3] else on_z
        at = began("4", ch, total.at[0 : len(line), 0:q, :])
        for _, to in line:
            send(at, total.at[z, rows, :], total.at[z, rows, :], to)

    def c5(ch):
        arrived("4", ch)
        n = CHUNKS[ch][2]
        if CHUNKS[ch][3]:
            at = began("5", ch, total.at[0 : NZ - 1, 0:n, :])
            for _, to in on_z:
                send(at, total.at[z, rows_of(ch), :], total.at[z, rows_of(ch), :], to)
        else:
            at = began("5", ch, total.at[:, 0 : 3 * n // NX, :])
            for _, to in on_x:
                send(at, total.at[:, quarter(ch, 0), :], total.at[:, quarter(ch, 0), :], to)

    outs = []

    def c6(ch):
        arrived("5", ch)
        copy = pltpu.make_async_copy(
            total.at[:, rows_of(ch), :], total_hbm.at[:, rows_of(ch), :], out_sem.at[2 + ch]
        )
        copy.start()
        outs.append(copy)

    tile = pl.ds(my_tile, 8)

    def gram_plane(ch):
        received(ex_core, g_core)
        folded[pl.ds(mine, half_rows)] += g_core[...]
        at = began("f", -1, g_plane)
        for d, (other, to) in enumerate(on_plane):
            src = folded.at[pl.ds(pl.multiple_of(c * half_rows + other * 8, 8), 8)]
            send(at, src, g_plane.at[d], to)

    def gram_line(ch):
        arrived("f", -1)
        g_line[z] = folded[tile, :] + summed(g_plane, NX * NY - 1)
        at = began("g", -1, g_plane.at[0 : NZ - 1])
        for _, to in on_z:
            send(at, g_line.at[z], g_line.at[z], to)

    def gram_spread(ch):
        arrived("g", -1)
        g_sum[tile, :] = summed(g_line, NZ)
        at = began("h", -1, g_plane)
        for _, to in on_plane:
            send(at, g_sum.at[tile], g_sum.at[tile], to)

    def gram_core(ch):
        arrived("h", -1)
        at = began("i", -1, g_core)
        my_half = pl.ds(mine, half_rows)
        send(at, g_sum.at[my_half], g_sum.at[my_half], sibling)

    def gram_ready(ch):
        arrived("i", -1)
        mat[0:128, :] = g_sum[0:128, 0:k]
        mat[128:256, 128:] = g_sum[128:256, 0 : k - 128]
        mat[256:, 256:] = g_sum[128 : k - 128, 256 : k]

    def factor(i):
        factor_step(mat, block, i // 3, i % 3)

    def basis(ch):
        rows = lax.broadcasted_iota(jnp.int32, (k, k), 0)
        cols = lax.broadcasted_iota(jnp.int32, (k, k), 1)
        mat[...] = jnp.where(rows >= cols, mat[...], 0.0)
        basis_t[...] = jnp.dot(
            mat[...], sketch[...], precision=HIGHEST, preferred_element_type=F32
        ) * math.sqrt(n_total)
        for j, (src, dst) in enumerate(((mat, inv_hbm), (basis_t, basis_hbm))):
            copy = pltpu.make_async_copy(src, dst, out_sem.at[j])
            copy.start()
            outs.append(copy)

    steps = dict(
        ya=ya, yb=yb, y2=y2, y3=y3, xa=xa, xb=xb, x2=x2, za=za, zb=zb, z2=z2, z3=z3, c4=c4, c5=c5, c6=c6,
        gram_plane=gram_plane, gram_line=gram_line, gram_spread=gram_spread, gram_core=gram_core,
        gram_ready=gram_ready, factor=factor, basis=basis,
    )
    for name, arg in ORDER:
        steps[name](arg)
    for copy in outs:
        copy.wait()
    for at, like in pending:
        wait_bytes(sems.at[at], like)


def finish_kernel(n_total, basis_in, total_ref, inv_ref, basis_out, coef_ref):
    basis_out[...] = basis_in[...]
    both = jnp.concatenate([total_ref[0], total_ref[1]], axis=1)
    coef_ref[...] = jnp.dot(
        inv_ref[...], both, precision=HIGHEST, preferred_element_type=F32
    ) * (1.0 / math.sqrt(n_total))


def per_device(activations, test_matrix):
    rows, d = activations.shape
    k = test_matrix.shape[1]
    n_total = rows * lax.axis_size("wide") * lax.axis_size("narrow")
    width = d // (2 * NY)
    bufs = []
    half = NZ // 2
    for axis, _, n, _ in CHUNKS:
        q = n // NX
        if axis == "y":
            shapes = ((2, half, n, LANES), (2, NZ, n, LANES), (3, NZ, q, LANES), (7, q, LANES))
        elif axis == "x":
            shapes = (
                (2, NY, half, q, LANES), (2, NY, NZ, q, LANES), (3, NZ, q, LANES), (7, q, LANES)
            )
        else:
            shapes = ((3, NY, n, LANES), (4, NY, n, LANES), (3, n, LANES), (3, q, LANES))
        bufs += [pltpu.VMEM(s, F32) for s in shapes]
    block = (NY, NZ, k, LANES)
    hbm = pl.BlockSpec(memory_space=pl.ANY)
    basis_t, total, inverse = pl.pallas_call(
        functools.partial(kernel, n_total),
        out_shape=(
            jax.ShapeDtypeStruct((k, rows), F32),
            jax.ShapeDtypeStruct((NZ, k, LANES), F32),
            jax.ShapeDtypeStruct((k, k), F32),
        ),
        in_specs=[hbm] * 2,
        out_specs=(hbm, hbm, hbm),
        scratch_shapes=[
            pltpu.VMEM((d // width, rows, width), BF16),
            pltpu.VMEM((d // width, k, width), BF16),
            pltpu.VMEM((k, rows), F32),
            pltpu.VMEM((k, 2 * rows), BF16),
            pltpu.VMEM(block, F32),
            pltpu.VMEM(block, F32),
            pltpu.VMEM(block, F32),
            pltpu.VMEM((NZ, k, LANES), F32),
            pltpu.VMEM((256, 384), F32),
            pltpu.VMEM((128, 384), F32),
            pltpu.VMEM((NX * NY - 1, 8, 384), F32),
            pltpu.VMEM((NZ, 8, 384), F32),
            pltpu.VMEM((256, 384), F32),
            pltpu.VMEM((k, k), F32),
            pltpu.VMEM((BLOCK, 2 * BLOCK), F32),
            pltpu.VMEM((k, rows), F32),
            pltpu.SemaphoreType.DMA((2 * d // width,)),
            pltpu.SemaphoreType.DMA((2 + len(CHUNKS),)),
            pltpu.SemaphoreType.DMA((SEMAPHORES,)),
        ] + bufs,
        compiler_params=pltpu.CompilerParams(
            collective_id=0, has_side_effects=True, vmem_limit_bytes=56 * 1024 * 1024
        ),
        name="range_finder",
    )(activations, test_matrix.T)
    steps = NZ // 2
    by_columns = pl.BlockSpec((k, rows // steps), lambda i: (0, i))
    basis_t, coeffs = pl.pallas_call(
        functools.partial(finish_kernel, n_total),
        grid=(steps,),
        out_shape=(
            jax.ShapeDtypeStruct((k, rows), F32),
            jax.ShapeDtypeStruct((k, width), F32),
        ),
        in_specs=[
            by_columns,
            pl.BlockSpec((2, k, LANES), lambda i: (i, 0, 0)),
            pl.BlockSpec((k, k), lambda i: (0, 0)),
        ],
        out_specs=(by_columns, pl.BlockSpec((k, 2 * LANES), lambda i: (0, i))),
        name="apply_inverse",
    )(basis_t, total, inverse)
    return basis_t.T, coeffs


def solution(mesh):
    return jax.shard_map(
        per_device,
        mesh=mesh,
        in_specs=(P(("wide", "narrow"), None), P()),
        out_specs=(P(("wide", "narrow"), None), P(None, "narrow")),
        check_vma=False,
    )
```

time: 82.2 us -> 75.4 us (0.917); the launches traced: 81.1 us -> 75.2 us
  Pallas kernels: 80.5 us -> 74.6 us
    pallas_call x1, Pallas kernels: 75.1 us -> 69.2 us  [per_device(): pl.pallas_call(functools.partial(kernel, n_total), out_shape=(jax.ShapeDt...]
where the time goes in v4:
time: 75.4 us; the launch traced here: 75.2 us
  Pallas kernels  74.6 us (99%)
    pallas_call x1, Pallas kernels, per_device(): pl.pallas_call(functools.partial(kernel, n_total), out_shape=(jax.ShapeDt...  69.2 us
    pallas_call x1, Pallas kernels, per_device(): pl.pallas_call(functools.partial(finish_kernel, n_total), grid=(steps,),...  5.32 us

profile of v4, /device:TPU:8, one launch (start us, length us, event | category | flops | bytes accessed | tf_op | source)
XLA Modules:
  0.0 75.2 jit_solution(13443157002696044936)
XLA Ops:
  0.6 69.2 %range_finder.1 = (f32[320,512]{1,0:T(8,128)}, f32[8,320,128]{2,1,0:T(8,128)}, f32[320,320]{1,0:T(8,128)}) custom-call(bf16[512,8192]{1,0:T(8,128)(2,1)} %a_hbm.1, bf16[320,8192]{1,0:T(8,128)(2,1)} %bitcast.2), custom_call_target="tpu_custom_call" | custom-call | tf_op jit(solution)/shard_map/range_finder/pallas_call | solution.py:482
  69.9 5.3 %apply_inverse.1 = (f32[320,512]{1,0:T(8,128)}, f32[320,1024]{1,0:T(8,128)}) custom-call(f32[320,512]{1,0:T(8,128)} %get-tuple-element.7.basis_in, f32[8,320,128]{2,1,0:T(8,128)} %get-tuple-element.8.total_ref, f32[320,320]{1,0:T(8,128)} %get-tuple-element.9.inv_ref), custom_call_target="tpu_custom_call" | custom-call | tf_op jit(solution)/shard_map/apply_inverse/pallas_call | solution.py:519

commit v5 on v4

--- a/solution.py
+++ b/solution.py
@@ -16,34 +16,39 @@
 BLOCK = 64
 LANES = 128
 SEMAPHORES = 176
-BEFORE_GRAM = 3
+BEFORE_GRAM = 4
 
 CHUNKS = (
-    ("y", 0, 32, True),
-    ("x", 32, 32, False),
+    ("z", 0, 32, False),
+    ("y", 32, 32, False),
     ("x", 64, 32, False),
-    ("y", 96, 32, False),
-    ("y", 128, 32, True),
-    ("x", 160, 32, False),
-    ("z", 192, 32, False),
-    ("x", 224, 32, False),
-    ("z", 256, 32, False),
+    ("z", 96, 32, False),
+    ("x", 128, 32, False),
+    ("y", 160, 32, True),
+    ("x", 192, 32, False),
+    ("z", 224, 32, False),
+    ("x", 256, 32, False),
     ("y", 288, 32, True),
 )
 
 ORDER = (
-    ("ya", 0), ("xa", 1), ("xa", 2), ("gram_plane", -1), ("ya", 3), ("ya", 4), ("xa", 5), ("yb", 0),
-    ("xb", 1), ("za", 6), ("xa", 7), ("xb", 2), ("za", 8), ("yb", 3), ("gram_line", -1), ("ya", 9), ("yb", 4),
-    ("xb", 5), ("y2", 0), ("zb", 6), ("x2", 1), ("xb", 7), ("y2", 3), ("zb", 8), ("yb", 9), ("x2", 2),
-    ("gram_spread", -1), ("y2", 4), ("x2", 5), ("y3", 1), ("y3", 0), ("z2", 6), ("y2", 9), ("x2", 7),
-    ("y3", 2), ("y3", 3), ("z2", 8), ("gram_core", -1), ("y3", 5), ("y3", 4), ("z3", 6), ("c4", 1), ("c4", 0),
-    ("gram_ready", -1), ("y3", 7), ("y3", 9), ("factor", 0), ("c4", 2), ("z3", 8), ("factor", 1), ("c4", 3),
-    ("c4", 6), ("factor", 2), ("c4", 5), ("c5", 0), ("c4", 4), ("factor", 3), ("c5", 1), ("c4", 7), ("c4", 8),
-    ("factor", 4), ("c4", 9), ("c5", 2), ("factor", 5), ("c5", 3), ("c5", 4), ("c5", 6), ("factor", 6),
-    ("c5", 5), ("factor", 7), ("c6", 1), ("c5", 9), ("factor", 8), ("factor", 9), ("c5", 7), ("c6", 0),
-    ("c6", 2), ("factor", 10), ("c6", 3), ("c5", 8), ("factor", 11), ("c6", 6), ("factor", 12),
-    ("factor", 13), ("c6", 5), ("c6", 4), ("factor", 14), ("basis", -1), ("c6", 7), ("c6", 9), ("c6", 8),
+    ("za", 0), ("gram_start", -1), ("ya", 1), ("xa", 2), ("za", 3), ("gram_plane", -1), ("xa", 4), ("ya", 5),
+    ("xa", 6), ("zb", 0), ("yb", 1), ("za", 7), ("xb", 2), ("xa", 8), ("ya", 9), ("gram_line", -1), ("zb", 3),
+    ("xb", 4), ("yb", 5), ("xb", 6), ("y2", 1), ("x2", 2), ("z2", 0), ("yb", 9), ("xb", 8), ("zb", 7),
+    ("y2", 5), ("x2", 4), ("y3", 2), ("z3", 0), ("gram_spread", -1), ("x2", 6), ("y3", 1), ("y2", 9),
+    ("z2", 3), ("y3", 4), ("x2", 8), ("y3", 5), ("c4", 0), ("y3", 6), ("z2", 7), ("z3", 3), ("gram_core", -1),
+    ("y3", 9), ("c4", 2), ("c4", 1), ("y3", 8), ("gram_ready", -1), ("c4", 4), ("factor", 0), ("factor", 1),
+    ("z3", 7), ("c5", 0), ("c4", 5), ("c4", 3), ("c4", 6), ("factor", 2), ("factor", 3), ("c4", 9), ("c5", 2),
+    ("factor", 4), ("c5", 1), ("c4", 7), ("c4", 8), ("factor", 5), ("c5", 4), ("c6", 0), ("c5", 5),
+    ("factor", 6), ("c5", 9), ("c5", 3), ("c5", 6), ("factor", 7), ("c6", 2), ("factor", 8), ("factor", 9),
+    ("c6", 1), ("c5", 7), ("factor", 10), ("c5", 8), ("c6", 4), ("factor", 11), ("factor", 12), ("c6", 3),
+    ("factor", 13), ("c6", 6), ("c6", 5), ("factor", 14), ("basis", -1), ("c6", 7), ("c6", 9), ("c6", 8),
 )
+
+
+def split(value):
+    high = value.astype(BF16)
+    return high, (value - high.astype(F32)).astype(BF16)
 
 
 def eliminate(state, first, last):
@@ -175,22 +180,23 @@
             sketch[...] += term
 
     value = sketch[...]
-    high = value.astype(BF16)
-    low = (value - high.astype(F32)).astype(BF16)
+    high, low = split(value)
     halves[:, 0:rows_here] = high
     halves[:, rows_here:] = low
 
-    def project(block, dst, at):
+    def project(block, dst, at, first):
+        rows = pl.ds(first, k // 2)
         cols = a_buf[block]
         res = jnp.dot(
-            halves[...], jnp.concatenate([cols, cols], axis=0), preferred_element_type=F32
+            halves[rows, :], jnp.concatenate([cols, cols], axis=0), preferred_element_type=F32
         )
         for t in range(NZ):
-            dst[at, t] = res[:, t * LANES : (t + 1) * LANES]
-
-    pl.semaphore_wait(barrier, len(partners))
-    for o in range(NY):
-        project(2 * o + 1 - c, to_core, o)
+            dst[at, t, rows, :] = res[:, t * LANES : (t + 1) * LANES]
+
+    def project_half(mine, first):
+        for o in range(NY):
+            project(2 * o + (c if mine else 1 - c), part if mine else to_core, o, first)
+
     ex_chunk = []
 
     def to_sibling(chunks):
@@ -200,24 +206,28 @@
             ex_chunk.append(at)
             send(at, to_core.at[:, :, rows, :], from_core.at[:, :, rows, :], sibling)
 
+    project_half(False, 0)
+    pl.semaphore_wait(barrier, len(partners))
     to_sibling(CHUNKS[:BEFORE_GRAM])
-
-    gram = lax.dot_general(
-        sketch[...], sketch[...], (((1,), (1,)), ((), ())),
-        precision=HIGHEST, preferred_element_type=F32,
-    )
-    folded[...] = jnp.zeros(folded.shape, F32)
-    folded[0:128, 0:k] = gram[0:128, :]
-    folded[128:256, 0 : k - 128] = gram[128:256, 128:]
-    folded[128 : k - 128, 256 : k] = gram[256:, 256:]
+    project_half(True, 0)
+    project_half(False, k // 2)
+
     half_rows = g_core.shape[0]
     mine = pl.multiple_of(c * half_rows, 8)
     yours = pl.multiple_of((1 - c) * half_rows, 8)
-    ex_core = exchange(g_core)
-    send(ex_core, folded.at[pl.ds(yours, half_rows)], g_core, sibling)
-    to_sibling(CHUNKS[BEFORE_GRAM:])
-    for o in range(NY):
-        project(2 * o + c, part, o)
+
+    def gram_start(ch):
+        gram = lax.dot_general(
+            sketch[...], sketch[...], (((1,), (1,)), ((), ())),
+            precision=HIGHEST, preferred_element_type=F32,
+        )
+        folded[...] = jnp.zeros(folded.shape, F32)
+        folded[0:128, 0:k] = gram[0:128, :]
+        folded[128:256, 0 : k - 128] = gram[128:256, 128:]
+        folded[128 : k - 128, 256 : k] = gram[256:, 256:]
+        send(began("e", -1, g_core), folded.at[pl.ds(yours, half_rows)], g_core, sibling)
+        to_sibling(CHUNKS[BEFORE_GRAM:])
+        project_half(True, k // 2)
 
     my_tile = pl.multiple_of(c * half_rows + place * 8, 8)
 
@@ -390,7 +400,7 @@
     tile = pl.ds(my_tile, 8)
 
     def gram_plane(ch):
-        received(ex_core, g_core)
+        arrived("e", -1)
         folded[pl.ds(mine, half_rows)] += g_core[...]
         at = began("f", -1, g_plane)
         for d, (other, to) in enumerate(on_plane):
@@ -440,8 +450,8 @@
 
     steps = dict(
         ya=ya, yb=yb, y2=y2, y3=y3, xa=xa, xb=xb, x2=x2, za=za, zb=zb, z2=z2, z3=z3, c4=c4, c5=c5, c6=c6,
-        gram_plane=gram_plane, gram_line=gram_line, gram_spread=gram_spread, gram_core=gram_core,
-        gram_ready=gram_ready, factor=factor, basis=basis,
+        gram_start=gram_start, gram_plane=gram_plane, gram_line=gram_line, gram_spread=gram_spread,
+        gram_core=gram_core, gram_ready=gram_ready, factor=factor, basis=basis,
     )
     for name, arg in ORDER:
         steps[name](arg)
@@ -453,9 +463,13 @@
 
 def finish_kernel(n_total, basis_in, total_ref, inv_ref, basis_out, coef_ref):
     basis_out[...] = basis_in[...]
-    both = jnp.concatenate([total_ref[0], total_ref[1]], axis=1)
+    tiles = total_ref.shape[0]
+    inv_high, inv_low = split(inv_ref[...])
+    high, low = split(jnp.concatenate([total_ref[t] for t in range(tiles)], axis=1))
     coef_ref[...] = jnp.dot(
-        inv_ref[...], both, precision=HIGHEST, preferred_element_type=F32
+        jnp.concatenate([inv_high, inv_low, inv_high], axis=1),
+        jnp.concatenate([high, high, low], axis=0),
+        preferred_element_type=F32,
     ) * (1.0 / math.sqrt(n_total))
 
 
@@ -514,7 +528,7 @@
         ),
         name="range_finder",
     )(activations, test_matrix.T)
-    steps = NZ // 2
+    steps = 2
     by_columns = pl.BlockSpec((k, rows // steps), lambda i: (0, i))
     basis_t, coeffs = pl.pallas_call(
         functools.partial(finish_kernel, n_total),
@@ -525,10 +539,10 @@
         ),
         in_specs=[
             by_columns,
-            pl.BlockSpec((2, k, LANES), lambda i: (i, 0, 0)),
+            pl.BlockSpec((NZ // steps, k, LANES), lambda i: (i, 0, 0)),
             pl.BlockSpec((k, k), lambda i: (0, 0)),
         ],
-        out_specs=(by_columns, pl.BlockSpec((k, 2 * LANES), lambda i: (0, i))),
+        out_specs=(by_columns, pl.BlockSpec((k, width // steps), lambda i: (0, i))),
         name="apply_inverse",
     )(basis_t, total, inverse)
     return basis_t.T, coeffs

time: 75.4 us -> 70.9 us (0.940)
  Pallas kernels: 74.6 us -> 69.4 us
    pallas_call x1, Pallas kernels: 69.2 us -> 66.1 us  [per_device(): pl.pallas_call(functools.partial(kernel, n_total), out_shape=(jax.ShapeDt...]
    pallas_call x1, Pallas kernels: 5.32 us -> 3.31 us  [per_device(): pl.pallas_call(functools.partial(finish_kernel, n_total), grid=(steps,),...]
where the time goes in v5:
time: 70.9 us; the launch traced here: 70 us
  Pallas kernels  69.4 us (98%)
    pallas_call x1, Pallas kernels, per_device(): pl.pallas_call(functools.partial(kernel, n_total), out_shape=(jax.ShapeDt...  66.1 us
    pallas_call x1, Pallas kernels, per_device(): pl.pallas_call(functools.partial(finish_kernel, n_total), grid=(steps,),...  3.31 us

profile of v5, /device:TPU:8, one launch (start us, length us, event | category | flops | bytes accessed | tf_op | source)
XLA Modules:
  0.0 70.0 jit_solution(8777650658515112071)
XLA Ops:
  0.6 66.1 %range_finder.1 = (f32[320,512]{1,0:T(8,128)}, f32[8,320,128]{2,1,0:T(8,128)}, f32[320,320]{1,0:T(8,128)}) custom-call(bf16[512,8192]{1,0:T(8,128)(2,1)} %a_hbm.1, bf16[320,8192]{1,0:T(8,128)(2,1)} %bitcast.2), custom_call_target="tpu_custom_call" | custom-call | tf_op jit(solution)/shard_map/range_finder/pallas_call | solution.py:496
  66.7 3.3 %apply_inverse.1 = (f32[320,512]{1,0:T(8,128)}, f32[320,1024]{1,0:T(8,128)}) custom-call(f32[320,512]{1,0:T(8,128)} %get-tuple-element.7.basis_in, f32[8,320,128]{2,1,0:T(8,128)} %get-tuple-element.8.total_ref, f32[320,320]{1,0:T(8,128)} %get-tuple-element.9.inv_ref), custom_call_target="tpu_custom_call" | custom-call | tf_op jit(solution)/shard_map/apply_inverse/pallas_call | solution.py:533

commit v6 on v5

--- a/solution.py
+++ b/solution.py
@@ -16,6 +16,7 @@
 BLOCK = 64
 LANES = 128
 SEMAPHORES = 176
+LAST_STEPS = 5
 BEFORE_GRAM = 4
 
 CHUNKS = (
@@ -134,6 +135,7 @@
 
     used = [0]
     pending = []
+    late = []
 
     def exchange(size_like):
         at = used[0]
@@ -244,6 +246,8 @@
 
     def began(name, ch, like):
         at = exchange(like)
+        if name in ("4", "5"):
+            late.append(at)
         flying[name, ch] = (at, like)
         return at
 
@@ -453,7 +457,12 @@
         gram_start=gram_start, gram_plane=gram_plane, gram_line=gram_line, gram_spread=gram_spread,
         gram_core=gram_core, gram_ready=gram_ready, factor=factor, basis=basis,
     )
-    for name, arg in ORDER:
+    for at_step, (name, arg) in enumerate(ORDER):
+        if at_step == len(ORDER) - LAST_STEPS:
+            early = [p for p in pending if p[0] not in late]
+            for at, like in early:
+                wait_bytes(sems.at[at], like)
+            pending[:] = [p for p in pending if p[0] in late]
         steps[name](arg)
     for copy in outs:
         copy.wait()

time: 70.9 us -> 70.8 us (level)
  no operation moved by 1% of the time
where the time goes in v6:
time: 70.8 us; the launch traced here: 69.9 us
  Pallas kernels  69.3 us (98%)
    pallas_call x1, Pallas kernels, per_device(): pl.pallas_call(functools.partial(kernel, n_total), out_shape=(jax.ShapeDt...  66 us
    pallas_call x1, Pallas kernels, per_device(): pl.pallas_call(functools.partial(finish_kernel, n_total), grid=(steps,),...  3.31 us

profile of v6, /device:TPU:8, one launch (start us, length us, event | category | flops | bytes accessed | tf_op | source)
XLA Modules:
  0.0 69.9 jit_solution(7735133497720617667)
XLA Ops:
  0.6 66.0 %range_finder.1 = (f32[320,512]{1,0:T(8,128)}, f32[8,320,128]{2,1,0:T(8,128)}, f32[320,320]{1,0:T(8,128)}) custom-call(bf16[512,8192]{1,0:T(8,128)(2,1)} %a_hbm.1, bf16[320,8192]{1,0:T(8,128)(2,1)} %bitcast.2), custom_call_target="tpu_custom_call" | custom-call | tf_op jit(solution)/shard_map/range_finder/pallas_call | solution.py:505
  66.6 3.3 %apply_inverse.1 = (f32[320,512]{1,0:T(8,128)}, f32[320,1024]{1,0:T(8,128)}) custom-call(f32[320,512]{1,0:T(8,128)} %get-tuple-element.7.basis_in, f32[8,320,128]{2,1,0:T(8,128)} %get-tuple-element.8.total_ref, f32[320,320]{1,0:T(8,128)} %get-tuple-element.9.inv_ref), custom_call_target="tpu_custom_call" | custom-call | tf_op jit(solution)/shard_map/apply_inverse/pallas_call | solution.py:542
